TPU v7x, 128 devices: a whole 4x4x4 slice. The times are simulated.
128 devices in a mesh: dom: 128 (over z, x, y, core).
Axes of the slice: x: 4, y: 4, z: 4, core: 2. Of those that a mesh axis runs over, the one named last changes fastest.
Arguments:
- elem_dofs: float32 [56, 9, 32768], P(None, None, 'dom'), may hold values from -6 to 6
- star_mats: float32 [3, 9, 9, 32768], P(None, None, None, 'dom'), may hold values from -1.25 to 1.25
- flux_solver: float32 [2, 4, 9, 9, 32768], P(None, None, None, None, 'dom'), may hold values from -1.5 to 1.5
- stiffness: float32 [3, 56, 56], replicated, may hold values from -0.75 to 0.75
- face_proj: float32 [4, 21, 56], replicated, may hold values from -0.75 to 0.75
- lift_mats: float32 [4, 56, 21], replicated, may hold values from -0.625 to 0.625
- neighbours: int32 [4, 32768], P(None, 'dom'), may hold values from 0 to 32895, as said below
- neighbour_face: int32 [4, 32768], P(None, 'dom'), may hold values from 0 to 3
- cluster: int32 [32768], P('dom'), may hold values from 0 to 3
- fault_elem: int32 [32768], P('dom'), may hold values from 0 to 255, as said below
- fault_face: int32 [32768], P('dom'), may hold values from 0 to 3, as said below
- fault_target: int32 [32768], P('dom'), may hold values from -1 to 32767, as said below
- fault_params: float32 [3, 21, 32768], P(None, None, 'dom'), may hold values from 0.2 to 12, as said below
- fault_state: float32 [21, 32768], P(None, 'dom'), may hold values from 1 to 3
Outputs:
- updated_dofs: float32 [56, 9, 32768], P(None, None, 'dom')
- slip_rate: float32 [21, 32768], P(None, 'dom')
- updated_state: float32 [21, 32768], P(None, 'dom')
Inputs may be any that keep to these rules, and one draw needn't show every extreme that they name: `neighbours`: for an element of device i the number lies in [i * 256, (i + 1) * 256 + 2 * 64), and is never the element's own; both ends are reached. `fault_elem`: on each device the live slots name distinct pairs of element and face. `fault_face`: on each device the live slots name distinct pairs of element and face. `fault_target`: A live slot's value t names owner device t // 256 and slot t % 256 there; no t appears twice; on each device the live slots come first, at least three quarters of them, and some device has all 256 live. At most 2 live slots of one device share an owner, and some device sends exactly 2 to some owner; each owner receives from at most 128 devices. `fault_params`: row 0 lies in 0.2 to 0.6, row 1 in 1.5 to 12, row 2 in 0.5 to 2.
All inputs are finite; a program needn't handle non-finite values.
Results may differ from a plain program's by a relative error of at most 0.0003.
Values sent between devices are 32-bit elements; how exact they have to be, the bound alone decides.
A program may use at most 128 MiB of HBM per device.

v0:
```python
import jax
import jax.numpy as jnp
from jax import lax
from jax.sharding import PartitionSpec as P

ORD = 6
NF = 4
NC = 4
NEWTON = 4


exact_mode = lax.Precision.HIGHEST
base_step = 0.2
steady_state = 0.8


def with_halo(block, sides, width):
    for axis, dim in sides:
        count = lax.axis_size(axis)
        forward = [(i, i + 1) for i in range(count - 1)]
        backward = [(target, source) for source, target in forward]
        low = lax.ppermute(
            lax.slice_in_dim(block, block.shape[dim] - width, None, axis=dim), axis, forward
        )
        high = lax.ppermute(lax.slice_in_dim(block, 0, width, axis=dim), axis, backward)
        block = jnp.concatenate([low, block, high], axis=dim)
    return block


def inverse_sinh(value):
    magnitude = jnp.abs(value)
    result = jnp.log(magnitude + jnp.sqrt(1.0 + magnitude * magnitude))
    return jnp.where(value < 0.0, -result, result)


def derivatives(elem_dofs, stiffness, star_mats):
    node_count, comp_count, elem_count = elem_dofs.shape
    stacked = stiffness.reshape(3 * node_count, node_count)
    taylor = [elem_dofs]
    for degree in range(ORD - 1):
        stiffened = jnp.dot(
            stacked,
            taylor[-1].reshape(node_count, comp_count * elem_count),
            precision=exact_mode,
            preferred_element_type=jnp.float32,
        )
        stiffened = stiffened.reshape(3, node_count, comp_count, elem_count)
        taylor.append(
            jnp.sum(star_mats[:, None, :, :, :] * stiffened[:, :, None, :, :], axis=(0, 3))
        )
    return jnp.stack(taylor)


def integrate(taylor):
    levels_out = []
    for level_id in range(NC):
        interval = base_step * 2.0**level_id
        weight = 1.0
        summed = jnp.zeros(taylor.shape[1:], jnp.float32)
        for degree in range(ORD):
            weight = weight * interval / (degree + 1)
            summed = summed + weight * taylor[degree]
        levels_out.append(summed)
    return jnp.stack(levels_out, axis=1)


def face_values(
    elem_dofs,
    star_mats,
    stiffness,
    face_proj,
    cluster,
    neighbours,
    neighbour_face,
    own_int,
    ext_int,
    offset,
):
    node_count, comp_count, elem_count = elem_dofs.shape
    face_pts = face_proj.shape[1]
    ext_count = ext_int.shape[3]
    lengths = jnp.array([base_step * 2.0**level_id for level_id in range(NC)], jnp.float32)
    selector = (cluster[None, :] == jnp.arange(NC, dtype=jnp.int32)[:, None]).astype(jnp.float32)
    elem_step = jnp.sum(selector * lengths[:, None], axis=0)
    own_sum = jnp.sum(own_int * selector[None, :, None, :], axis=1)
    flipped = jnp.transpose(stiffness, (0, 2, 1)).reshape(3 * node_count, node_count)
    stiffened = jnp.dot(
        flipped,
        own_sum.reshape(node_count, comp_count * elem_count),
        precision=exact_mode,
        preferred_element_type=jnp.float32,
    )
    stiffened = stiffened.reshape(3, node_count, comp_count, elem_count)
    volume = jnp.sum(star_mats[:, None, :, :, :] * stiffened[:, :, None, :, :], axis=(0, 3))
    projector = face_proj.reshape(NF * face_pts, node_count)
    own_face = jnp.dot(
        projector,
        own_sum.reshape(node_count, comp_count * elem_count),
        precision=exact_mode,
        preferred_element_type=jnp.float32,
    )
    own_face = own_face.reshape(NF, face_pts, comp_count, elem_count)
    face_table = jnp.dot(
        projector,
        ext_int.reshape(node_count, NC * comp_count * ext_count),
        precision=exact_mode,
        preferred_element_type=jnp.float32,
    )
    face_table = face_table.reshape(NF, face_pts, NC, comp_count, ext_count).transpose(
        1, 3, 0, 2, 4
    )
    face_table = face_table.reshape(face_pts * comp_count, NF * NC * ext_count)
    column = (neighbour_face * NC + cluster[None, :]) * ext_count + (neighbours - offset)
    nb_face = jnp.take(face_table, column.reshape(-1), axis=1)
    nb_face = nb_face.reshape(face_pts, comp_count, NF, elem_count).transpose(2, 0, 1, 3)
    return (elem_step, volume, own_face, nb_face)


def fault_traces(own_face, nb_face, elem_step, fault_elem, fault_face):
    fault_step = elem_step[fault_elem]
    inner_side = jnp.transpose(own_face[fault_face, :, :, fault_elem], (2, 1, 0)) / fault_step
    outer_side = jnp.transpose(nb_face[fault_face, :, :, fault_elem], (2, 1, 0)) / fault_step
    return (inner_side, outer_side, fault_step)


def friction(near_rows, far_rows, params, state_var):
    rate_coef, stress_bg, impedance = (params[0], params[1], params[2])
    locked = 0.5 * (near_rows[1] + far_rows[1]) + impedance * (far_rows[2] - near_rows[2])
    normal = jnp.maximum(stress_bg - 0.5 * (near_rows[0] + far_rows[0]), 1.0)
    strength = normal * rate_coef
    state_gain = 0.5 * jnp.exp(state_var)
    slip_value = jnp.zeros_like(locked)
    for turn in range(NEWTON):
        scaled = state_gain * slip_value
        mismatch = impedance * slip_value + strength * inverse_sinh(scaled) - locked
        tangent = impedance + strength * state_gain / jnp.sqrt(1.0 + scaled * scaled)
        slip_value = slip_value - mismatch / tangent
    traction = locked - impedance * slip_value
    state_next = steady_state + (state_var - steady_state) * jnp.exp(-jnp.abs(slip_value))
    return (traction, slip_value, state_next)


def finish(
    elem_dofs,
    flux_solver,
    lift_mats,
    volume,
    own_face,
    nb_face,
    inner_side,
    outer_side,
    fault_step,
    traction,
    slip_value,
    fault_elem,
    fault_face,
    is_live,
):
    node_count, comp_count, elem_count = elem_dofs.shape
    face_pts = own_face.shape[1]
    imposed = outer_side.at[3].set(traction).at[7].set(inner_side[7] + slip_value)
    imposed = jnp.transpose(imposed * fault_step, (2, 1, 0))
    face_slot = jnp.where(is_live, fault_face, NF)
    nb_face = nb_face.at[face_slot, :, :, fault_elem].set(imposed, mode="drop")
    face_flux = jnp.sum(flux_solver[0][:, None] * own_face[:, :, None], axis=3) + jnp.sum(
        flux_solver[1][:, None] * nb_face[:, :, None], axis=3
    )
    lifting = jnp.transpose(lift_mats, (1, 0, 2)).reshape(node_count, NF * face_pts)
    surface = jnp.dot(
        lifting,
        face_flux.reshape(NF * face_pts, comp_count * elem_count),
        precision=exact_mode,
        preferred_element_type=jnp.float32,
    )
    return elem_dofs + volume - surface.reshape(node_count, comp_count, elem_count)


def local(
    elem_dofs,
    star_mats,
    flux_solver,
    stiffness,
    face_proj,
    lift_mats,
    neighbours,
    neighbour_face,
    cluster,
    fault_elem,
    fault_face,
    fault_target,
    fault_params,
    fault_state,
):
    node_count, comp_count, elem_count = elem_dofs.shape
    rim_width = elem_count // 4
    device = lax.axis_index("dom")
    device_count = lax.axis_size("dom")
    taylor = derivatives(elem_dofs, stiffness, star_mats)
    ext_taylor = with_halo(taylor, (("dom", 3),), rim_width)
    ext_int = integrate(ext_taylor)
    own_int = ext_int[:, :, :, rim_width : rim_width + elem_count]
    elem_step, volume, own_face, nb_face = face_values(
        elem_dofs,
        star_mats,
        stiffness,
        face_proj,
        cluster,
        neighbours,
        neighbour_face,
        own_int,
        ext_int,
        device * elem_count,
    )
    is_live = fault_target >= 0
    inner_side, outer_side, fault_step = fault_traces(
        own_face, nb_face, elem_step, fault_elem, fault_face
    )
    slot_total = fault_target.shape[0]
    face_pts = inner_side.shape[1]
    slot_cap = max(2, slot_total // device_count)
    owner_dev = jnp.where(is_live, fault_target // slot_total, device_count)
    member = (owner_dev[:, None] == jnp.arange(device_count, dtype=jnp.int32)[None, :]).astype(
        jnp.int32
    )
    rank_in = jnp.sum((jnp.cumsum(member, axis=0) - member) * member, axis=1)
    buffer_len = device_count * slot_cap
    position = jnp.where(is_live, owner_dev * slot_cap + rank_in, buffer_len)
    slot_buffer = (
        jnp.full((1, 1, buffer_len), -1, jnp.int32)
        .at[0, 0, position]
        .set(fault_target % slot_total, mode="drop")
    )
    payload = jnp.concatenate([inner_side, outer_side])
    sending = (
        jnp.zeros((2 * comp_count, face_pts, buffer_len), jnp.float32)
        .at[:, :, position]
        .set(payload, mode="drop")
    )
    received, slot_recv = (
        lax.all_to_all(sending, "dom", split_axis=2, concat_axis=2, tiled=True),
        lax.all_to_all(slot_buffer, "dom", split_axis=2, concat_axis=2, tiled=True),
    )
    near_rows = jnp.stack([received[0], received[3], received[7]])
    far_rows = jnp.stack([received[comp_count], received[comp_count + 3], received[comp_count + 7]])
    owned_slot = slot_recv[0, 0]
    safe_slot = jnp.clip(owned_slot, 0, slot_total - 1)
    traction_owner, slip_owner, state_next = friction(
        near_rows, far_rows, fault_params[:, :, safe_slot], fault_state[:, safe_slot]
    )
    updated_state = fault_state.at[:, jnp.where(owned_slot >= 0, owned_slot, slot_total)].set(
        state_next, mode="drop"
    )
    returned = lax.all_to_all(
        jnp.stack([traction_owner, slip_owner]), "dom", split_axis=2, concat_axis=2, tiled=True
    )
    picked = jnp.take(returned, jnp.minimum(position, buffer_len - 1), axis=2)
    traction = jnp.where(is_live, picked[0], 0.0)
    slip_rate = jnp.where(is_live, picked[1], 0.0)
    updated_dofs = finish(
        elem_dofs,
        flux_solver,
        lift_mats,
        volume,
        own_face,
        nb_face,
        inner_side,
        outer_side,
        fault_step,
        traction,
        slip_rate,
        fault_elem,
        fault_face,
        is_live,
    )
    return (updated_dofs, slip_rate, updated_state)


def solution(mesh):
    return jax.shard_map(
        local,
        mesh=mesh,
        in_specs=(
            P(None, None, "dom"),
            P(None, None, None, "dom"),
            P(None, None, None, None, "dom"),
            P(),
            P(),
            P(),
            P(None, "dom"),
            P(None, "dom"),
            P("dom"),
            P("dom"),
            P("dom"),
            P("dom"),
            P(None, None, "dom"),
            P(None, "dom"),
        ),
        out_specs=(P(None, None, "dom"), P(None, "dom"), P(None, "dom")),
        check_vma=False,
    )
```

profile of v0, /device:TPU:1, one launch (start us, length us, event | category | flops | bytes accessed | tf_op | source)
XLA Modules:
  0.0 350.5 jit_solution(11778662194521092035)
XLA Ops:
  8.1 3.2 mul.710
  17.9 2.9 mul.713
  27.3 2.9 mul.716
  36.6 12.4 %mul.719 = f32[3,56,9,256]{3,2,1,0:T(8,128)} reshape(f32[168,2304]{1,0:T(8,128)} %convolution_bitcast_fusion.2) | data formatting | bytes 3096576 | tf_op jit(solution)/shard_map/mul | solution.py:49
  55.6 3.5 collective-permute-start.1
  59.1 3.2 collective-permute-start
  65.8 13.6 %all-to-all-start.1 = ((s32[1,1,256]{1,0,2:T(1,128)}), s32[1,1,256]{1,0,2:T(1,128)S(1)}, u32[]{:S(2)}, u32[]{:S(2)}) async-start(s32[1,1,256]{1,0,2:T(1,128)} %copy.258), calls=%async_computation.1 | async-start | bytes 262144 | tf_op jit(solution)/shard_map/all_to_all | solution.py:241
  94.2 4.6 %reduce.4 = s32[256]{0:T(256)S(1)} reduce(s32[1,1,256]{1,0,2:T(1,128)S(1)} %all-to-all-done.1, s32[]{:T(128)} %constant.184.clone.1), dimensions={0,1}, to_apply=%all_to_all.10.reduce_sub_computation | reduce | bytes 2052 | tf_op jit(solution)/shard_map/all_to_all | solution.py:241
  99.4 4.1 %pad_maximum_fusion = f32[6,56,9,384]{3,1,2,0:T(8,128)S(1)} fusion(f32[6,56,9,64]{3,1,2,0:T(8,128)S(1)} %collective-permute-done.1, f32[6,56,9,256]{3,1,2,0:T(8,128)} %copy-done, f32[6,56,9,64]{3,1,2,0:T(8,128)} %collective-permute-done), kind=kLoop, calls=%fused_computation.21 | loop fusion | flops 2322432 | bytes 9289728 | tf_op jit(solution)/shard_map/concatenate | solution.py:26
  105.0 3.2 copy.245
  108.2 5.2 %reshape.724 = f32[56,13824]{1,0:T(8,128)} reshape(f32[56,4,9,384]{3,2,1,0:T(8,128)} %copy.245) | data formatting | bytes 6193152 | tf_op jit(solution)/shard_map/reshape | solution.py:105
  113.4 8.1 %convolution_bitcast_fusion = f32[84,13824]{1,0:T(8,128)} fusion(f32[56,13824]{1,0:T(8,128)} %reshape.724, f32[84,56]{1,0:T(8,128)} %reshape.723), kind=kOutput, calls=%fused_computation.11 | convolution fusion | flops 780337152 | bytes 7760256 | tf_op jit(solution)/shard_map/dot_general | solution.py:103
  121.5 6.8 %reshape.725 = f32[4,21,4,9,384]{4,3,2,1,0:T(8,128)} reshape(f32[84,13824]{1,0:T(8,128)} %convolution_bitcast_fusion) | data formatting | bytes 9289728 | tf_op jit(solution)/shard_map/reshape | solution.py:109
  128.3 7.3 %copy.246 = f32[21,9,4,4,384]{4,3,2,1,0:T(4,128)} copy(f32[21,9,4,4,384]{4,1,3,0,2:T(8,128)} %bitcast.352) | data formatting | bytes 9289728 | tf_op jit(solution)/shard_map/transpose | solution.py:109
  135.6 6.0 %reshape.726 = f32[189,6144]{1,0:T(8,128)} reshape(f32[21,9,4,4,384]{4,3,2,1,0:T(4,128)} %copy.246) | data formatting | bytes 9289728 | tf_op jit(solution)/shard_map/reshape | solution.py:112
  141.7 6.2 %copy.247 = f32[189,6144]{0,1:T(8,128)} copy(f32[189,6144]{1,0:T(8,128)} %reshape.726) | data formatting | bytes 9289728 | tf_op jit(solution)/shard_map/reshape | solution.py:112
  147.9 7.4 %gather_fusion = f32[1024,189]{1,0:T(8,128)} fusion(f32[189,6144]{0,1:T(8,128)} %copy.247, s32[1024]{0:T(1024)S(1)} %broadcast_clamp_fusion), kind=kCustom, calls=%fused_computation | custom fusion | bytes 1552384 | tf_op jit(solution)/shard_map/jit(_take)/gather | solution.py:114
  160.1 5.9 %copy.249 = f32[21,9,4,256]{0,1,3,2:T(8,128)} copy(f32[21,9,4,256]{3,2,1,0:T(4,128)} %gather.26) | data formatting | bytes 1548288 | tf_op jit(solution)/shard_map/jit(_take)/gather | solution.py:114
  169.9 6.8 %copy.253 = f32[4,21,9,256]{1,2,3,0:T(8,128)} copy(f32[4,21,9,256]{3,2,1,0:T(8,128)S(1)} %mul.785) | data formatting | bytes 1548288 | tf_op jit(solution)/shard_map/mul | solution.py:165
  176.6 4.5 %gather_fusion.3 = f32[256,21,9]{1,2,0:T(8,128)S(1)} fusion(f32[4,21,9,256]{1,2,3,0:T(8,128)} %copy.253, s32[256]{0:T(256)S(1)} %bitcast.350), kind=kCustom, calls=%fused_computation.3 | custom fusion | bytes 389120 | tf_op jit(solution)/shard_map/gather | solution.py:121
  182.6 7.4 %select_bitcast_fusion = f32[4,21,9,256]{1,2,3,0:T(8,128)} fusion(f32[21,9,4,256]{0,1,3,2:T(8,128)} %copy.249, pred[4,256]{1,0:T(4,128)(4,1)S(1)} %copy-done.29), kind=kLoop, calls=%fused_computation.18 | loop fusion | flops 193536 | bytes 1549312 | tf_op jit(solution)/shard_map/transpose | solution.py:115
  190.0 4.5 %gather_fusion.1 = f32[256,21,9]{1,2,0:T(8,128)S(1)} fusion(f32[4,21,9,256]{1,2,3,0:T(8,128)} %select_bitcast_fusion, s32[256]{0:T(256)S(1)} %bitcast.351), kind=kCustom, calls=%fused_computation.1 | custom fusion | bytes 389120 | tf_op jit(solution)/shard_map/gather | solution.py:122
  201.4 32.9 %scatter_fusion = f32[18,21,256]{1,0,2:T(8,128)} fusion(f32[18,21,256]{1,0,2:T(8,128)} %broadcast_in_dim.93, s32[256]{0:T(256)S(1)} %copy-done.28, f32[256,18,21]{2,1,0:T(8,128)} %copy.255), kind=kCustom, calls=%fused_computation.7 | custom fusion | bytes 1162240 | tf_op jit(solution)/shard_map/scatter | solution.py:237
  234.3 4.1 %reshape.845 = f32[128,1,756]{2,1,0:T(1,128)} reshape(f32[256,18,21]{2,1,0:T(8,128)} %bitcast.354) | data formatting | bytes 774144
  238.4 9.9 %all-to-all-start = ((f32[128,1,756]{2,1,0:T(1,128)}), f32[128,1,756]{2,1,0:T(1,128)}, u32[]{:S(2)}, u32[]{:S(2)}) async-start(f32[128,1,756]{2,1,0:T(1,128)} %reshape.845), calls=%async_computation | async-start | bytes 786432 | tf_op jit(solution)/shard_map/all_to_all | solution.py:240
  263.4 3.2 reshape.846
  266.6 4.4 %fusion.71 = (f32[1,21,256]{1,0,2:T(1,128)}, f32[1,21,256]{1,0,2:T(1,128)}, f32[1,21,256]{1,0,2:T(1,128)}, f32[1,21,256]{1,0,2:T(1,128)}, f32[1,21,256]{1,0,2:T(1,128)}, /*index=5*/f32[1,21,256]{1,0,2:T(1,128)}) fusion(f32[18,21,256]{1,0,2:T(8,128)} %bitcast.357), kind=kLoop, calls=%fused_computation.195 | loop fusion | bytes 258048 | tf_op jit(solution)/shard_map/slice | solution.py:244
  285.3 8.2 %all-to-all-start.2 = ((f32[2,21,256]{1,0,2:T(2,128)}), f32[2,21,256]{1,0,2:T(2,128)}, u32[]{:S(2)}, u32[]{:S(2)}) async-start(f32[2,21,256]{1,0,2:T(2,128)} %copy.267), calls=%async_computation.2 | async-start | bytes 524288 | tf_op jit(solution)/shard_map/all_to_all | solution.py:253
  299.0 5.2 %all-to-all-done.2 = f32[2,21,256]{1,0,2:T(2,128)} async-done(((f32[2,21,256]{1,0,2:T(2,128)}), f32[2,21,256]{1,0,2:T(2,128)}, u32[]{:S(2)}, u32[]{:S(2)}) %all-to-all-start.2) | async-done | bytes 43040 | tf_op jit(solution)/shard_map/all_to_all | solution.py:253
  309.8 27.0 %scatter_fusion.1 = f32[4,21,9,256]{1,2,3,0:T(8,128)} fusion(f32[4,21,9,256]{1,2,3,0:T(8,128)} %select_bitcast_fusion, s32[256]{0:T(256)S(1)} %bitcast.353, f32[256,21,9]{1,2,0:T(8,128)S(1)} %copy.269), kind=kCustom, calls=%fused_computation.9 | custom fusion | bytes 582656 | tf_op jit(solution)/shard_map/scatter | solution.py:164
  336.8 5.9 %copy.270 = f32[4,21,9,256]{3,0,2,1:T(4,128)S(1)} copy(f32[4,21,9,256]{1,2,3,0:T(8,128)} %scatter_fusion.1) | data formatting | bytes 1548288 | tf_op jit(solution)/shard_map/scatter | solution.py:164
  342.7 4.8 %multiply_reduce_fusion.6 = (f32[4,21,9,256]{3,0,2,1:T(4,128)S(1)}, f32[4,21,9,256]{3,0,2,1:T(4,128)S(1)}) fusion(f32[4,21,9,256]{3,0,2,1:T(4,128)S(1)} %copy.270, f32[4,9,9,256]{3,0,2,1:T(4,128)S(1)} %copy-done.14, f32[4,21,9,256]{3,0,2,1:T(4,128)S(1)} %copy.244, f32[4,9,9,256]{3,0,2,1:T(4,128)S(1)} %copy-done.15), kind=kLoop, calls=%fused_computation.19 | loop fusion | flops 6580224 | bytes 3760128 | tf_op jit(solution)/shard_map/reduce_sum | solution.py:165
  (182 shorter events, 113.5 us)
Async XLA Ops:
  0.6 3.6 %copy-start.19 = (f32[3,9,9,256]{3,0,2,1:T(4,128)S(1)}, f32[3,9,9,256]{3,0,2,1:T(4,128)}, u32[]{:S(2)}) copy-start(f32[3,9,9,256]{3,0,2,1:T(4,128)} %param.20) | copy-start | bytes 746500
  4.2 1.4 copy-start.6
  53.0 2.6 copy-start
  53.0 9.3 %copy-start.31 = (s32[256]{0:T(256)S(1)}, s32[256]{0:T(256)}, u32[]{:S(2)}) copy-start(s32[256]{0:T(256)} %param.30) | copy-start | bytes 3076
  53.0 26.4 %copy-start.24 = (s32[4,256]{1,0:T(4,128)S(1)}, s32[4,256]{1,0:T(4,128)}, u32[]{:S(2)}) copy-start(s32[4,256]{1,0:T(4,128)} %param.25) | copy-start | bytes 12292
  53.0 26.4 %copy-start.25 = (s32[4,256]{1,0:T(4,128)S(1)}, s32[4,256]{1,0:T(4,128)}, u32[]{:S(2)}) copy-start(s32[4,256]{1,0:T(4,128)} %param.26) | copy-start | bytes 12292
  55.6 33.7 %copy-start.22 = (f32[21,256]{1,0:T(8,128)S(1)}, f32[21,256]{1,0:T(8,128)}, u32[]{:S(2)}) copy-start(f32[21,256]{1,0:T(8,128)} %param.32) | copy-start | bytes 64516
  55.6 34.5 %copy-start.21 = (f32[4,56,21]{1,0,2:T(4,128)S(1)}, f32[4,56,21]{1,0,2:T(4,128)}, u32[]{:S(2)}) copy-start(f32[4,56,21]{1,0,2:T(4,128)} %param.24) | copy-start | bytes 56452
  55.6 35.1 %copy-start.10 = (f32[3,56,56]{2,1,0:T(8,128)S(1)}, f32[3,56,56]{2,1,0:T(8,128)}, u32[]{:S(2)}) copy-start(f32[3,56,56]{2,1,0:T(8,128)} %param.22) | copy-start | bytes 112900
  55.6 43.8 %collective-permute-start.1 = (f32[6,56,9,64]{3,1,2,0:T(8,128)}, f32[6,56,9,64]{3,1,2,0:T(8,128)S(1)}, u32[]{:S(2)}, u32[]{:S(2)}) collective-permute-start(f32[6,56,9,64]{3,1,2,0:T(8,128)} %get-tuple-element.63), channel_id=1, source_target_pairs={{1,0},{2,1},{3,2},{4,3},{5,4},{6,5},{7,6},{8,7},{9,8},{10,9},{11,1... | collective-permute-start | bytes 2322440 | tf_op jit(solution)/shard_map/ppermute | solution.py:25
  59.1 40.3 %collective-permute-start = (f32[6,56,9,64]{3,1,2,0:T(8,128)}, f32[6,56,9,64]{3,1,2,0:T(8,128)}, u32[]{:S(2)}, u32[]{:S(2)}) collective-permute-start(f32[6,56,9,64]{3,1,2,0:T(8,128)} %get-tuple-element.62), channel_id=1, source_target_pairs={{0,1},{1,2},{2,3},{3,4},{4,5},{5,6},{6,7},{7,8},{8,9},{9,10},{10,1... | collective-permute-start | bytes 2322440 | tf_op jit(solution)/shard_map/ppermute | solution.py:22
  63.6 15.8 %copy-start.27 = (s32[256]{0:T(256)}, s32[256]{0:T(256)S(1)}, u32[]{:S(2)}) copy-start(s32[256]{0:T(256)S(1)} %get-tuple-element.77) | copy-start | bytes 3076
  65.8 28.4 %all-to-all-start.1 = ((s32[1,1,256]{1,0,2:T(1,128)}), s32[1,1,256]{1,0,2:T(1,128)S(1)}, u32[]{:S(2)}, u32[]{:S(2)}) async-start(s32[1,1,256]{1,0,2:T(1,128)} %copy.258), calls=%async_computation.1 | async-start | bytes 262144 | tf_op jit(solution)/shard_map/all_to_all | solution.py:241
  160.1 5.9 %copy-start.23 = (f32[4,256]{1,0:T(4,128)S(1)}, f32[4,256]{1,0:T(4,128)}, u32[]{:S(2)}) copy-start(f32[4,256]{1,0:T(4,128)} %get-tuple-element.76) | copy-start | bytes 12292
  169.8 6.8 %copy-start.1 = (f32[4,21,9,256]{3,2,1,0:T(8,128)}, f32[4,21,9,256]{3,2,1,0:T(8,128)S(1)}, u32[]{:S(2)}) copy-start(f32[4,21,9,256]{3,2,1,0:T(8,128)S(1)} %mul.785) | copy-start | bytes 2322436
  176.6 6.0 %copy-start.29 = (pred[4,256]{1,0:T(4,128)(4,1)S(1)}, pred[4,256]{1,0:T(4,128)(4,1)}, u32[]{:S(2)}) copy-start(pred[4,256]{1,0:T(4,128)(4,1)} %get-tuple-element.75) | copy-start | bytes 3076
  190.0 6.0 %copy-start.26 = (f32[256]{0:T(256)S(1)}, f32[256]{0:T(256)}, u32[]{:S(2)}) copy-start(f32[256]{0:T(256)} %gather_fusion.2) | copy-start | bytes 3076
  197.1 2.4 copy-start.16
  197.1 4.3 %copy-start.12 = (f32[9,21,256]{2,1,0:T(8,128)}, f32[9,21,256]{2,1,0:T(8,128)S(1)}, u32[]{:S(2)}) copy-start(f32[9,21,256]{2,1,0:T(8,128)S(1)} %get-tuple-element.69) | copy-start | bytes 580612
  197.1 4.3 %copy-start.28 = (s32[256]{0:T(256)S(1)}, s32[256]{0:T(256)}, u32[]{:S(2)}) copy-start(s32[256]{0:T(256)} %copy-done.27) | copy-start | bytes 3076
  201.4 46.9 %copy-start.30 = (s32[256,1]{0,1:T(1,128)S(1)}, s32[256,1]{0,1:T(1,128)}, u32[]{:S(2)}) copy-start(s32[256,1]{0,1:T(1,128)} %get-tuple-element.67) | copy-start | bytes 3076
  201.4 49.8 %copy-start.5 = (f32[21,256]{0,1:T(8,128)S(1)}, f32[21,256]{0,1:T(8,128)}, u32[]{:S(2)}) copy-start(f32[21,256]{0,1:T(8,128)} %copy.265) | copy-start | bytes 64516
  201.4 50.6 %copy-start.18 = (f32[3,56,56]{2,1,0:T(8,128)S(1)}, f32[3,56,56]{2,1,0:T(8,128)}, u32[]{:S(2)}) copy-start(f32[3,56,56]{2,1,0:T(8,128)} %copy.241) | copy-start | bytes 112900
  238.4 21.9 %all-to-all-start = ((f32[128,1,756]{2,1,0:T(1,128)}), f32[128,1,756]{2,1,0:T(1,128)}, u32[]{:S(2)}, u32[]{:S(2)}) async-start(f32[128,1,756]{2,1,0:T(1,128)} %reshape.845), calls=%async_computation | async-start | bytes 786432 | tf_op jit(solution)/shard_map/all_to_all | solution.py:240
  263.3 30.2 %copy-start.3 = (f32[3,56,9,256]{3,1,2,0:T(8,128)S(1)}, f32[3,56,9,256]{3,1,2,0:T(8,128)}, u32[]{:S(2)}) copy-start(f32[3,56,9,256]{3,1,2,0:T(8,128)} %copy.242) | copy-start | bytes 4644868
  266.6 29.0 %copy-start.2 = (f32[4,21,9,256]{3,2,1,0:T(8,128)S(1)}, f32[4,21,9,256]{3,2,1,0:T(8,128)}, u32[]{:S(2)}) copy-start(f32[4,21,9,256]{3,2,1,0:T(8,128)} %copy-done.1) | copy-start | bytes 2322436
  285.3 18.9 %all-to-all-start.2 = ((f32[2,21,256]{1,0,2:T(2,128)}), f32[2,21,256]{1,0,2:T(2,128)}, u32[]{:S(2)}, u32[]{:S(2)}) async-start(f32[2,21,256]{1,0,2:T(2,128)} %copy.267), calls=%async_computation.2 | async-start | bytes 524288 | tf_op jit(solution)/shard_map/all_to_all | solution.py:253
  295.5 11.6 %copy-start.13 = (f32[9,21,256]{2,1,0:T(8,128)S(1)}, f32[9,21,256]{2,1,0:T(8,128)}, u32[]{:S(2)}) copy-start(f32[9,21,256]{2,1,0:T(8,128)} %copy-done.12) | copy-start | bytes 580612
  336.8 5.9 %copy-start.14 = (f32[4,9,9,256]{3,0,2,1:T(4,128)S(1)}, f32[4,9,9,256]{3,0,2,1:T(4,128)}, u32[]{:S(2)}) copy-start(f32[4,9,9,256]{3,0,2,1:T(4,128)} %get-tuple-element.64) | copy-start | bytes 995332
  336.8 5.9 %copy-start.15 = (f32[4,9,9,256]{3,0,2,1:T(4,128)S(1)}, f32[4,9,9,256]{3,0,2,1:T(4,128)}, u32[]{:S(2)}) copy-start(f32[4,9,9,256]{3,0,2,1:T(4,128)} %get-tuple-element.65) | copy-start | bytes 995332
  347.9 1.4 copy-start.4
  347.9 1.4 copy-start.11
  (5 other events, 5.8 us)
where the time goes:
time: 357 us; the launch traced here: 350 us
  local copies, waits for them, and re-layouts  230 us (64%)
  other arithmetic  47.4 us (13%)
  starting transfers between devices  38.4 us (11%)
  matrix products  25.4 us (7%)
  waiting for transfers between devices  7.47 us (2%)
    scatter x1, local copies, waits for them, and re-layouts, local(): sending = jnp.zeros((2 * comp_count, face_pts, buffer_len), jnp.float32)....  32.9 us
    scatter x2, local copies, waits for them, and re-layouts, finish(): nb_face = nb_face.at[face_slot, :, :, fault_elem].set(imposed, mode='drop')  32.9 us
    mul x8, local copies, waits for them, and re-layouts, derivatives(): star_mats[:, None, :, :, :] * stiffened[:, :, None, :, :]  32.1 us
    unnamed x86, local copies, waits for them, and re-layouts  23.4 us
    gather x4, local copies, waits for them, and re-layouts, face_values(): nb_face = jnp.take(face_table, column.reshape(-1), axis=1)  18.2 us
    all_to_all x1, starting transfers between devices, local(): lax.all_to_all(slot_buffer, 'dom', split_axis=2, concat_axis=2, tiled=True)  13.6 us
    dot_general x5, matrix products, derivatives(): jnp.dot(stacked, taylor[-1].reshape(node_count, comp_count * elem_count),...  12.4 us
    reshape x2, local copies, waits for them, and re-layouts, face_values(): face_table = face_table.reshape(face_pts * comp_count, NF * NC * ext_count)  12.3 us
  transfers between devices with their start and end apart: 5, of which 3 were waited for; matrix products, arithmetic and copies ran while one was open for 11% of the time, Pallas kernels for 0%

commit v1 on v0

v1 whole, which is shorter than its diff:
```python
import functools

import jax
import jax.numpy as jnp
from jax import lax
from jax.experimental import pallas as pl
from jax.experimental.pallas import tpu as pltpu
from jax.sharding import PartitionSpec as P

F32, BF16, I32 = jnp.float32, jnp.bfloat16, jnp.int32
MESH = pl.DeviceIdType.MESH
B, Q, FB, ORD, NF, NC, NEWTON = 56, 9, 21, 6, 4, 4, 4
E, RIM = 256, 64
LO, HI = 8, 16
GP = 32
EXT = 384
BASE_STEP, STEADY = 0.2, 0.8
TAUS = [BASE_STEP * 2.0**c for c in range(NC)]


def term_weights(tau):
    out, weight = [], 1.0
    for degree in range(ORD):
        weight = weight * tau / (degree + 1)
        out.append(weight)
    return out


WEIGHTS = [term_weights(tau) for tau in TAUS]


def iota(shape, dim):
    return lax.broadcasted_iota(I32, shape, dim)


def dot(a, b):
    return jnp.dot(a, b, preferred_element_type=F32)


def dot_nt(a, b):
    return lax.dot_general(a, b, (((1,), (1,)), ((), ())), preferred_element_type=F32)


def split2(x):
    high = x.astype(BF16).astype(F32)
    return high, x - high


def split3(x):
    high = x.astype(BF16)
    rest = x - high.astype(F32)
    mid = rest.astype(BF16)
    low = (rest - mid.astype(F32)).astype(BF16)
    return high, mid, low


def stacked(x):
    high, low = split2(x)
    gap = jnp.zeros((8, x.shape[1]), F32)
    half = jnp.concatenate([high, gap, low, gap], axis=0).astype(BF16)
    return jnp.concatenate([half, half], axis=0)


def left_factor(w):
    both = w + pltpu.roll(w, 64, axis=1)
    high, low = split2(both)
    return jnp.concatenate([high.astype(BF16), low.astype(BF16)], axis=1)


def inverse_sinh(value):
    magnitude = jnp.abs(value)
    result = jnp.log(magnitude + jnp.sqrt(1.0 + magnitude * magnitude))
    return jnp.where(value < 0.0, -result, result)


def kernel(
    dofs_h, star_h, flux_h, stiff, proj, lift, nbr, nbr_face, cluster, f_elem, f_face, f_target, params, state,
    out_h, slip_out, state_out,
    x, star, flux, st, wide, pad_sq, s4, st4, f4, l2, mem, own_of, etab, ubuf,
    hsl, hsr, hrl, hrr, halo, amat, gmat, y, of, nb, fx, acc, pp,
    bq, mq, mq2, rq, bp, mp, mp2, rp, bs, ms, ms2, rs,
    in_sem, out_sem, hs_sem, hr_sem, lo_s, lo_r, hi_s, hi_r,
):
    me = lax.axis_index("dom")
    hi, lo = me // LO, me % LO
    n = LO * HI
    left, right = (me + n - 1) % n, (me + 1) % n

    in_copies = [
        pltpu.make_async_copy(dofs_h, x.at[0], in_sem.at[0]),
        pltpu.make_async_copy(star_h, star, in_sem.at[1]),
        pltpu.make_async_copy(flux_h, flux, in_sem.at[2]),
    ]
    for copy in in_copies:
        copy.start()

    barrier = pltpu.get_barrier_semaphore()

    def greet_lo(j, _):
        pl.semaphore_signal(barrier, inc=1, device_id=(hi * LO + (lo + j) % LO,), device_id_type=MESH)
        return 0

    def greet_hi(j, _):
        pl.semaphore_signal(barrier, inc=1, device_id=(((hi + j) % HI) * LO + lo,), device_id_type=MESH)
        return 0

    lax.fori_loop(1, LO, greet_lo, 0)
    lax.fori_loop(1, HI, greet_hi, 0)
    pl.semaphore_signal(barrier, inc=1, device_id=(left,), device_id_type=MESH)
    pl.semaphore_signal(barrier, inc=1, device_id=(right,), device_id_type=MESH)

    def lo_copy(buf, dst, rows, which, j):
        t = (lo + j) % LO
        return pltpu.make_async_remote_copy(
            src_ref=buf.at[pl.ds(pl.multiple_of(t * rows, 8), rows)],
            dst_ref=dst.at[pl.ds(pl.multiple_of(lo * rows, 8), rows)],
            send_sem=lo_s.at[which, j], recv_sem=lo_r.at[which, j],
            device_id=(hi * LO + t,), device_id_type=MESH,
        )

    def hi_copy(buf, dst, rows, which, j):
        t = (hi + j) % HI
        return pltpu.make_async_remote_copy(
            src_ref=buf.at[pl.ds(pl.multiple_of(t * rows, 8), rows)],
            dst_ref=dst.at[pl.ds(pl.multiple_of(hi * rows, 8), rows)],
            send_sem=hi_s.at[which, j], recv_sem=hi_r.at[which, j],
            device_id=(t * LO + lo,), device_id_type=MESH,
        )

    def send(make, count, mine, buf, dst, rows, which):
        def one(j, _):
            make(buf, dst, rows, which, j).start()
            return 0

        lax.fori_loop(1, count, one, 0)
        block = pl.ds(pl.multiple_of(mine * rows, 8), rows)
        dst[block, :] = buf[block, :]

    def arrive(make, count, buf, dst, rows, which):
        def one(j, _):
            make(buf, dst, rows, which, j).wait_recv()
            return 0

        lax.fori_loop(1, count, one, 0)

    def sent(make, count, buf, dst, rows, which):
        def one(j, _):
            make(buf, dst, rows, which, j).wait_send()
            return 0

        lax.fori_loop(1, count, one, 0)

    def halo_copies(k):
        return (
            pltpu.make_async_remote_copy(
                src_ref=hsl.at[k], dst_ref=hrr.at[k], send_sem=hs_sem.at[0, k], recv_sem=hr_sem.at[0, k],
                device_id=(left,), device_id_type=MESH),
            pltpu.make_async_remote_copy(
                src_ref=hsr.at[k], dst_ref=hrl.at[k], send_sem=hs_sem.at[1, k], recv_sem=hr_sem.at[1, k],
                device_id=(right,), device_id_type=MESH),
        )

    wide[...] = jnp.zeros_like(wide)
    for d in range(3):
        wide[d * B : (d + 1) * B, 0:B] = stiff[d]
    s4[...] = left_factor(wide[...])
    for d in range(3):
        pad_sq[...] = jnp.zeros_like(pad_sq)
        pad_sq[0:B, 0:B] = stiff[d]
        wide[d * B : (d + 1) * B, :] = jnp.transpose(pad_sq[...])[0:B]
    st4[...] = left_factor(wide[...])
    pad_sq[...] = jnp.zeros_like(pad_sq)
    for f in range(NF):
        pad_sq[f * GP : f * GP + FB, 0:B] = proj[:, f, :]
    f4[...] = left_factor(pad_sq[...])
    pad_sq[...] = jnp.zeros_like(pad_sq)
    for f in range(NF):
        pad_sq[f * GP : f * GP + FB, 0:B] = lift[:, f, :]
    lift_high, lift_low = split2(jnp.transpose(pad_sq[...])[0:B])
    lift_rows = jnp.concatenate([lift_high, lift_low], axis=0).astype(BF16)
    l2[...] = jnp.concatenate([lift_rows, lift_rows], axis=1)
    fx[...] = jnp.zeros_like(fx)
    pp[...] = jnp.zeros_like(pp)
    for j in range(3):
        pp[24 * j : 24 * j + FB, :] = params[j]
    pp[72 : 72 + FB, :] = state[...]

    target = f_target[...]
    live = target >= 0
    owner = jnp.where(live, lax.shift_right_logical(target, 8), -1)
    slot = jnp.bitwise_and(target, E - 1)
    member = jnp.where(iota((n, E), 0) == owner, 1.0, 0.0)
    earlier = jnp.where(iota((E, E), 0) < iota((E, E), 1), 1.0, 0.0).astype(BF16)
    before = dot(member.astype(BF16), earlier)
    rank = jnp.sum(member * before, axis=0, keepdims=True)
    place = (jnp.bitwise_and(owner, LO - 1) * (2 * HI) + lax.shift_right_logical(owner, 3)).astype(F32) + HI * rank
    place = jnp.where(live, place, -1.0)
    mem[...] = jnp.where(iota((E, E), 0).astype(F32) == place, 1.0, 0.0).astype(BF16)
    grid_place = jnp.where(live, f_face[...] * E + f_elem[...], -1)
    for f in range(NF):
        etab[f * E : (f + 1) * E, :] = jnp.where(iota((E, E), 0) + f * E == grid_place, 1.0, 0.0).astype(BF16)
    ids = jnp.where(iota((128, E), 0) < 2, (slot + 1).astype(F32), 0.0).astype(BF16)
    asked = dot_nt(mem[...], ids).reshape(LO, 2, HI, 128)
    lane3 = iota((LO, HI, 128), 2)
    bq[...] = jnp.where(lane3 == 0, asked[:, 0], asked[:, 1]).reshape(n, 128)

    lane = iota((B, 128), 1)
    low_half = lane < RIM

    def pack_halo(k):
        def one(q, _):
            a, b = x[k, q, :, 0:128], x[k, jnp.minimum(q + 5, Q - 1), :, 0:128]
            hsl[k, q] = jnp.where(low_half, a, pltpu.roll(b, RIM, axis=1))
            a, b = x[k, q, :, 128:256], x[k, jnp.minimum(q + 5, Q - 1), :, 128:256]
            hsr[k, q] = jnp.where(low_half, pltpu.roll(a, RIM, axis=1), b)
            return 0

        lax.fori_loop(0, 5, one, 0)
        for copy in halo_copies(k):
            copy.start()

    def star_products(left_w, source):
        def one(q, _):
            st[q] = dot(left_w[...], stacked(source(q)))[0 : 3 * B]
            return 0

        lax.fori_loop(0, Q, one, 0, unroll=3)

    def star_sum(store):
        def one(g, _):
            for l in range(2):
                lanes = slice(l * 128, (l + 1) * 128)
                total = [jnp.zeros((B, 128), F32) for _ in range(3)]
                for q in range(Q):
                    for d in range(3):
                        value = st[q, d * B : (d + 1) * B, lanes]
                        for i in range(3):
                            total[i] = total[i] + star[g * 3 + i, q, d : d + 1, lanes] * value
                for i in range(3):
                    store(g * 3 + i, lanes, total[i])
            return 0

        lax.fori_loop(0, 3, one, 0)

    def taylor(k):
        star_products(s4, lambda q: x[k - 1, q])

        def store(p, lanes, value):
            x[k, p, :, lanes] = value

        star_sum(store)

    for copy in in_copies[:2]:
        copy.wait()
    pl.semaphore_wait(barrier, LO + HI)
    send(lo_copy, LO, lo, bq, mq, HI, 0)
    pack_halo(0)
    taylor(1)
    pack_halo(1)

    arrive(lo_copy, LO, bq, mq, HI, 0)
    for t in range(HI):
        mq2[t * LO : (t + 1) * LO, :] = mq[pl.ds(t, LO, stride=HI), :]
    send(hi_copy, HI, hi, mq2, rq, LO, 0)
    taylor(2)
    pack_halo(2)

    arrive(hi_copy, HI, mq2, rq, LO, 0)
    wanted = (iota((n, E), 1) + 1).astype(F32)
    for r in range(2):
        own_of[r * n : (r + 1) * n, :] = jnp.where(rq[:, r : r + 1] == wanted, 1.0, 0.0).astype(BF16)
    answer = sum(dot_nt(own_of[...], piece) for piece in split3(pp[...]))
    for t in range(HI):
        for r in range(2):
            bp[t * 16 + r * LO : t * 16 + (r + 1) * LO, :] = answer[r * n + t * LO : r * n + (t + 1) * LO]
    send(hi_copy, HI, hi, bp, mp, 16, 1)
    taylor(3)
    pack_halo(3)

    arrive(hi_copy, HI, bp, mp, 16, 1)
    for t in range(LO):
        for r in range(2):
            mp2[t * 32 + r * HI : t * 32 + (r + 1) * HI, :] = mp[pl.ds(r * LO + t, HI, stride=16), :]
    send(lo_copy, LO, lo, mp2, rp, 32, 1)
    taylor(4)
    pack_halo(4)
    taylor(5)
    pack_halo(5)

    level = cluster[...]

    def by_level(values):
        out = jnp.full((1, E), values[0], F32)
        for c in range(1, NC):
            out = jnp.where(level == c, values[c], out)
        return out

    step = by_level(TAUS)
    own_w = [by_level([WEIGHTS[c][k] for c in range(NC)]) for k in range(ORD)]

    def own_term(q, _):
        total = own_w[0] * x[0, q]
        for k in range(1, ORD):
            total = total + own_w[k] * x[k, q]
        wrapped = stacked(total)
        st[q] = dot(st4[...], wrapped)[0 : 3 * B]
        of[q] = dot(f4[...], wrapped)
        return 0

    lax.fori_loop(0, Q, own_term, 0)

    def store_volume(p, lanes, value):
        acc[p, :, lanes] = x[0, p, :, lanes] + value

    star_sum(store_volume)

    number = nbr[...] - me * E
    ext = jnp.where(number < RIM, number + E, jnp.where(number >= E + RIM, number, number - RIM))
    column = level * EXT + ext
    for f in range(NF):
        def build(c, _, f=f):
            rows = pl.ds(pl.multiple_of(c * E, E), E)
            hit = iota((E, E), 0) + c * E == column[f : f + 1]
            gmat[f, rows, :] = jnp.where(hit, 1.0, 0.0).astype(BF16)
            return 0

        lax.fori_loop(0, NC * EXT // E, build, 0)

    keep_low = jnp.where(me > 0, 1, 0)
    keep_high = jnp.where(me < n - 1, 1, 0)
    keep = jnp.where(lane < RIM, keep_low, keep_high) > 0
    for k in range(ORD):
        for copy in halo_copies(k):
            copy.wait_recv()

        def unpack(q, _, k=k):
            a, b = hrl[k, q], hrr[k, q]
            first = jnp.where(low_half, a, pltpu.roll(b, RIM, axis=1))
            halo[k, q] = jnp.where(keep, first, 0.0)
            second = jnp.where(low_half, pltpu.roll(a, RIM, axis=1), b)
            halo[k, q + 5] = jnp.where(keep, second, 0.0)
            return 0

        lax.fori_loop(0, 5, unpack, 0)

    def integrals(q, _):
        for l in range(3):
            if l < 2:
                terms = [x[k, q, :, l * 128 : (l + 1) * 128] for k in range(ORD)]
            else:
                terms = [halo[k, q] for k in range(ORD)]
            for c in range(NC):
                total = WEIGHTS[c][0] * terms[0]
                for k in range(1, ORD):
                    total = total + WEIGHTS[c][k] * terms[k]
                high, low = split2(total)
                rows = pl.ds(pl.multiple_of(q * 2 * B, 16), 2 * B)
                lanes = slice(c * EXT + l * 128, c * EXT + (l + 1) * 128)
                amat[rows, lanes] = jnp.concatenate([high, low], axis=0).astype(BF16)
        return 0

    lax.fori_loop(0, Q, integrals, 0)

    for f in range(NF):
        y[...] = dot(amat[...], gmat[f])
        side = nbr_face[f : f + 1, :]

        def project(q, _, f=f, side=side):
            base = pl.multiple_of(q * 2 * B, 8)
            value = y[pl.ds(base, B), :] + y[pl.ds(base + B, B), :]
            table = dot(f4[...], stacked(value))
            picked = table[0:24]
            for s in range(1, NF):
                picked = jnp.where(side == s, table[s * GP : s * GP + 24], picked)
            nb[q, f * GP : f * GP + 24, :] = picked
            return 0

        lax.fori_loop(0, Q, project, 0, unroll=3)

    arrive(lo_copy, LO, mp2, rp, 32, 1)
    by_slot = sum(dot(piece, mem[...]) for piece in split3(jnp.transpose(rp[...])))
    by_slot = jnp.where(iota((128, E), 0) == 96, 1.0, by_slot)
    slot_state = by_slot[72:96]
    slot_pieces = split3(by_slot)
    slips = []
    for f in range(NF):
        table = etab[f * E : (f + 1) * E, :]
        grid = sum(dot_nt(piece, table) for piece in slot_pieces)
        rate, stress, imp, var = grid[0:24], grid[24:48], grid[48:72], grid[72:96]
        here = grid[96:97] > 0.5
        imp = jnp.where(imp > 0.0, imp, 1.0)
        rows = slice(f * GP, f * GP + 24)
        inner = [of[p, rows, :] / step for p in (0, 3, 7)]
        outer = [nb[p, rows, :] / step for p in (0, 3, 7)]
        locked = 0.5 * (inner[1] + outer[1]) + imp * (outer[2] - inner[2])
        normal = jnp.maximum(stress - 0.5 * (inner[0] + outer[0]), 1.0)
        strength = normal * rate
        gain = 0.5 * jnp.exp(var)
        slip = jnp.zeros_like(locked)
        for _ in range(NEWTON):
            scaled = gain * slip
            mismatch = imp * slip + strength * inverse_sinh(scaled) - locked
            tangent = imp + strength * gain / jnp.sqrt(1.0 + scaled * scaled)
            slip = slip - mismatch / tangent
        traction = locked - imp * slip
        nb[3, rows, :] = jnp.where(here, step * traction, nb[3, rows, :])
        nb[7, rows, :] = jnp.where(here, step * (inner[2] + slip), nb[7, rows, :])
        slips.append(split3(jnp.where(here, slip, 0.0)))
    slot_slip = jnp.zeros((24, E), F32)
    for f in range(NF):
        for piece in slips[f]:
            slot_slip = slot_slip + dot(piece, etab[f * E : (f + 1) * E, :])
    slip_out[...] = slot_slip[0:FB]
    next_state = STEADY + (slot_state - STEADY) * jnp.exp(-jnp.abs(slot_slip))
    gap8, gap72 = jnp.zeros((8, E), F32), jnp.zeros((72, E), F32)
    wrapped = jnp.concatenate([next_state, gap8, next_state, gap72], axis=0)
    told = sum(dot_nt(mem[...], piece) for piece in split3(wrapped)).reshape(LO, 2, HI, 128)
    bs[...] = jnp.where(lane3 < 32, told[:, 0], told[:, 1]).reshape(n, 128)
    send(lo_copy, LO, lo, bs, ms, HI, 2)

    in_copies[2].wait()

    def fluxes(g, _):
        for l in range(2):
            lanes = slice(l * 128, (l + 1) * 128)
            for f in range(NF):
                rows = slice(f * GP, f * GP + 24)
                total = [jnp.zeros((24, 128), F32) for _ in range(3)]
                for q in range(Q):
                    mine, other = of[q, rows, lanes], nb[q, rows, lanes]
                    for i in range(3):
                        total[i] = total[i] + flux[0, g * 3 + i, q, f : f + 1, lanes] * mine
                        total[i] = total[i] + flux[1, g * 3 + i, q, f : f + 1, lanes] * other
                for i in range(3):
                    fx[g * 3 + i, rows, lanes] = total[i]
        return 0

    lax.fori_loop(0, 3, fluxes, 0)

    arrive(lo_copy, LO, bs, ms, HI, 2)
    for t in range(HI):
        ms2[t * LO : (t + 1) * LO, :] = ms[pl.ds(t, LO, stride=HI), :]
    send(hi_copy, HI, hi, ms2, rs, LO, 2)

    def lifted(p, _):
        high, low = split2(fx[p])
        both = jnp.concatenate([high, low], axis=0).astype(BF16)
        surface = dot(l2[...], both)
        acc[p] = acc[p] - (surface[0:B] + surface[B : 2 * B])
        return 0

    lax.fori_loop(0, Q, lifted, 0, unroll=3)
    out_copy = pltpu.make_async_copy(acc, out_h, out_sem)
    out_copy.start()

    arrive(hi_copy, HI, ms2, rs, LO, 2)
    turned = jnp.transpose(rs[...])
    news = jnp.concatenate([turned[0:24], turned[32:56]], axis=1)
    update = sum(dot(piece, own_of[...]) for piece in split3(news))
    hit = dot(jnp.ones((16, E), BF16), own_of[...])[0:1] > 0.5
    state_out[...] = jnp.where(hit, update[0:FB], state[...])

    sent(lo_copy, LO, bq, mq, HI, 0)
    sent(hi_copy, HI, mq2, rq, LO, 0)
    sent(hi_copy, HI, bp, mp, 16, 1)
    sent(lo_copy, LO, mp2, rp, 32, 1)
    sent(lo_copy, LO, bs, ms, HI, 2)
    sent(hi_copy, HI, ms2, rs, LO, 2)
    for k in range(ORD):
        for copy in halo_copies(k):
            copy.wait_send()
    out_copy.wait()


def local(*args):
    (elem_dofs, star_mats, flux_solver, stiffness, face_proj, lift_mats, neighbours, neighbour_face,
     cluster, fault_elem, fault_face, fault_target, fault_params, fault_state) = args
    vmem, anywhere = pl.BlockSpec(memory_space=pltpu.VMEM), pl.BlockSpec(memory_space=pl.ANY)
    halo = pltpu.VMEM((ORD, 5, B, 128), F32)
    small = pltpu.VMEM((LO * HI, 128), F32)
    double = pltpu.VMEM((2 * LO * HI, 128), F32)
    faces = pltpu.VMEM((Q, NF * GP, E), F32)
    square = pltpu.VMEM((E, E), BF16)
    out, slip, state = pl.pallas_call(
        kernel,
        out_shape=(
            jax.ShapeDtypeStruct((Q, B, E), F32),
            jax.ShapeDtypeStruct((FB, E), F32),
            jax.ShapeDtypeStruct((FB, E), F32),
        ),
        in_specs=[anywhere] * 3 + [vmem] * 11,
        out_specs=(anywhere, vmem, vmem),
        scratch_shapes=[
            pltpu.VMEM((ORD, Q, B, E), F32),
            pltpu.VMEM((Q, Q, 3, E), F32),
            pltpu.VMEM((2, Q, Q, NF, E), F32),
            pltpu.VMEM((Q, 3 * B, E), F32),
            pltpu.VMEM((176, 128), F32),
            pltpu.VMEM((128, 128), F32),
            pltpu.VMEM((176, 256), BF16),
            pltpu.VMEM((176, 256), BF16),
            pltpu.VMEM((128, 256), BF16),
            pltpu.VMEM((112, 256), BF16),
            square,
            square,
            pltpu.VMEM((NF * E, E), BF16),
            pltpu.VMEM((8, 128), F32),
            halo, halo, halo, halo,
            pltpu.VMEM((ORD, 10, B, 128), F32),
            pltpu.VMEM((Q * 2 * B, NC * EXT), BF16),
            pltpu.VMEM((NF, NC * EXT, E), BF16),
            pltpu.VMEM((Q * 2 * B, E), F32),
            faces, faces, faces,
            pltpu.VMEM((Q, B, E), F32),
            pltpu.VMEM((128, E), F32),
            small, small, small, small,
            double, double, double, double,
            small, small, small, small,
            pltpu.SemaphoreType.DMA((3,)),
            pltpu.SemaphoreType.DMA,
            pltpu.SemaphoreType.DMA((2, ORD)),
            pltpu.SemaphoreType.DMA((2, ORD)),
            pltpu.SemaphoreType.DMA((3, LO)),
            pltpu.SemaphoreType.DMA((3, LO)),
            pltpu.SemaphoreType.DMA((3, HI)),
            pltpu.SemaphoreType.DMA((3, HI)),
        ],
        compiler_params=pltpu.CompilerParams(
            collective_id=0, has_side_effects=True, vmem_limit_bytes=48 * 1024 * 1024
        ),
    )(
        jnp.transpose(elem_dofs, (1, 0, 2)),
        jnp.transpose(star_mats, (1, 2, 0, 3)),
        jnp.transpose(flux_solver, (0, 2, 3, 1, 4)),
        stiffness,
        jnp.transpose(face_proj, (1, 0, 2)),
        jnp.transpose(lift_mats, (2, 0, 1)),
        neighbours,
        neighbour_face,
        cluster.reshape(1, E),
        fault_elem.reshape(1, E),
        fault_face.reshape(1, E),
        fault_target.reshape(1, E),
        fault_params,
        fault_state,
    )
    return jnp.transpose(out, (1, 0, 2)), slip, state


def solution(mesh):
    return jax.shard_map(
        local,
        mesh=mesh,
        in_specs=(
            P(None, None, "dom"),
            P(None, None, None, "dom"),
            P(None, None, None, None, "dom"),
            P(),
            P(),
            P(),
            P(None, "dom"),
            P(None, "dom"),
            P("dom"),
            P("dom"),
            P("dom"),
            P("dom"),
            P(None, None, "dom"),
            P(None, "dom"),
        ),
        out_specs=(P(None, None, "dom"), P(None, "dom"), P(None, "dom")),
        check_vma=False,
    )
```

time: 357 us -> 66.1 us (0.19); the launches traced: 350 us -> 65.6 us
  local copies, waits for them, and re-layouts: 230 us -> 9.89 us
  Pallas kernels: 0 us -> 55 us
  other arithmetic: 47.4 us -> 0 us
  starting transfers between devices: 38.4 us -> 0 us
  matrix products: 25.4 us -> 0 us
  waiting for transfers between devices: 7.47 us -> 0 us
    scatter x6 -> x0, local copies, waits for them, and re-layouts: 69.3 us -> none  [the longest x1 32.9 us: local(): sending = jnp.zeros((2 * comp_count, face_pts, buffer_len), jnp.float32)....]
    pallas_call x0 -> x1, Pallas kernels: none -> 55 us  [local(): pl.pallas_call(kernel, out_shape=(jax.ShapeDtypeStruct((Q, B, E), F32), j...]
    mul x14 -> x0, local copies, waits for them, and re-layouts: 46.4 us -> none  [the longest x8 32.1 us: derivatives(): star_mats[:, None, :, :, :] * stiffened[:, :, None, :, :]]
    gather x15 -> x0, local copies, waits for them, and re-layouts: 38.4 us -> none  [the longest x4 18.2 us: face_values(): nb_face = jnp.take(face_table, column.reshape(-1), axis=1)]
    all_to_all x3 -> x0, starting transfers between devices: 31.7 us -> none  [the longest x1 13.6 us: local(): lax.all_to_all(slot_buffer, 'dom', split_axis=2, concat_axis=2, tiled=True)]
    reshape x11 -> x0, local copies, waits for them, and re-layouts: 25.7 us -> none  [the longest x2 12.3 us: face_values(): face_table = face_table.reshape(face_pts * comp_count, NF * NC * ext_count)]
    dot_general x9 -> x0, matrix products: 25.4 us -> none  [the longest x5 12.4 us: derivatives(): jnp.dot(stacked, taylor[-1].reshape(node_count, comp_count * elem_count),...]
    reduce_sum x10 -> x0, other arithmetic: 14.5 us -> none  [the longest x5 6.17 us: derivatives(): jnp.sum(star_mats[:, None, :, :, :] * stiffened[:, :, None, :, :], axis=(...]
  transfers between devices with their start and end apart: 5 -> 0, of which waited for: 3 -> 0; matrix products, arithmetic and copies ran while one was open for 11% -> 0% of each run, Pallas kernels for 0% -> 0%
where the time goes in v1:
time: 66.1 us; the launch traced here: 65.6 us
  Pallas kernels  55 us (83%)
  local copies, waits for them, and re-layouts  9.89 us (15%)
  between operations  0.7 us (1%)
    pallas_call x1, Pallas kernels, local(): pl.pallas_call(kernel, out_shape=(jax.ShapeDtypeStruct((Q, B, E), F32), j...  55 us
    unnamed x31, local copies, waits for them, and re-layouts  9.89 us

profile of v1, /device:TPU:1, one launch (start us, length us, event | category | flops | bytes accessed | tf_op | source)
XLA Modules:
  0.0 65.6 jit_solution(9496545825422841626)
XLA Ops:
  0.6 0.0 copy-start.13
  0.6 0.0 copy-start.11
  0.7 0.0 copy-start.12
  0.7 0.0 copy-start.9
  0.7 0.0 copy-start.8
  0.7 0.0 copy-start.10
  0.7 0.6 copy-done.13
  1.3 0.0 copy-done.11
  1.3 0.0 copy-done.12
  1.3 0.0 copy-done.9
  1.4 0.0 copy-done.8
  1.4 0.0 copy-done.10
  1.4 0.0 copy-start
  1.4 1.1 %copy-done = f32[2,4,9,9,256]{4,1,3,2,0:T(4,128)S(1)} copy-done((f32[2,4,9,9,256]{4,1,3,2,0:T(4,128)S(1)}, f32[2,4,9,9,256]{4,1,3,2,0:T(4,128)}, u32[]{:S(2)}) %copy-start) | copy-done | bytes 663576
  2.5 0.0 copy-start.1
  2.5 1.0 %copy-done.1 = f32[56,9,256]{2,0,1:T(8,128)S(1)} copy-done((f32[56,9,256]{2,0,1:T(8,128)S(1)}, f32[56,9,256]{2,0,1:T(8,128)}, u32[]{:S(2)}) %copy-start.1) | copy-done | bytes 516120
  3.5 0.0 copy-start.2
  3.5 1.0 %copy-done.2 = f32[3,9,9,256]{3,0,2,1:T(4,128)S(1)} copy-done((f32[3,9,9,256]{3,0,2,1:T(4,128)S(1)}, f32[3,9,9,256]{3,0,2,1:T(4,128)}, u32[]{:S(2)}) %copy-start.2) | copy-done | bytes 248856
  4.5 0.0 copy-start.3
  4.5 0.9 %copy-done.3 = f32[3,56,56]{2,1,0:T(8,128)S(1)} copy-done((f32[3,56,56]{2,1,0:T(8,128)S(1)}, f32[3,56,56]{2,1,0:T(8,128)}, u32[]{:S(2)}) %copy-start.3) | copy-done | bytes 37656
  5.4 0.0 copy-start.4
  5.4 0.9 %copy-done.4 = f32[3,21,256]{2,1,0:T(8,128)S(1)} copy-done((f32[3,21,256]{2,1,0:T(8,128)S(1)}, f32[3,21,256]{2,1,0:T(8,128)}, u32[]{:S(2)}) %copy-start.4) | copy-done | bytes 64536
  6.3 0.0 copy-start.5
  6.3 0.8 %copy-done.5 = f32[4,21,56]{2,0,1:T(4,128)S(1)} copy-done((f32[4,21,56]{2,0,1:T(4,128)S(1)}, f32[4,21,56]{2,0,1:T(4,128)}, u32[]{:S(2)}) %copy-start.5) | copy-done | bytes 18840
  7.1 0.0 copy-start.6
  7.1 0.8 %copy-done.6 = f32[4,56,21]{1,0,2:T(4,128)S(1)} copy-done((f32[4,56,21]{1,0,2:T(4,128)S(1)}, f32[4,56,21]{1,0,2:T(4,128)}, u32[]{:S(2)}) %copy-start.6) | copy-done | bytes 18840
  7.8 0.0 copy-start.7
  7.8 0.7 %copy-done.7 = f32[21,256]{1,0:T(8,128)S(1)} copy-done((f32[21,256]{1,0:T(8,128)S(1)}, f32[21,256]{1,0:T(8,128)}, u32[]{:S(2)}) %copy-start.7) | copy-done | bytes 21528
  8.6 55.0 %shard_map.157 = (f32[9,56,256]{2,1,0:T(8,128)S(1)}, f32[21,256]{1,0:T(8,128)S(1)}, f32[21,256]{1,0:T(8,128)S(1)}) custom-call(f32[9,56,256]{2,1,0:T(8,128)S(1)} %bitcast.11, f32[9,9,3,256]{3,2,1,0:T(4,128)S(1)} %bitcast.13, f32[2,9,9,4,256]{4,3,2,1,0:T(4,128)S(1)} %bitcast.10, f32[3,56,56]{2,1,0:T(8,128)S(1)} %copy-done.3, f32[21,4,56]{2,1,0:T(4,128)S(1)} %bitcast.14, ...), custom_call_target="tpu_custom_call" | custom-call | tf_op jit(solution)/shard_map/pallas_call | solution.py:484
  63.6 0.8 %copy.20 = f32[56,9,256]{2,0,1:T(8,128)} copy(f32[56,9,256]{2,0,1:T(8,128)S(1)} %bitcast.12) | data formatting | bytes 1032192
  64.3 0.6 copy.21
  65.0 0.6 copy.22
Async XLA Ops:
  0.6 0.7 %copy-start.13 = (s32[256]{0:T(256)S(1)}, s32[256]{0:T(256)}, u32[]{:S(2)}) copy-start(s32[256]{0:T(256)} %param.25) | copy-start | bytes 3076
  0.6 0.7 %copy-start.11 = (s32[256]{0:T(256)S(1)}, s32[256]{0:T(256)}, u32[]{:S(2)}) copy-start(s32[256]{0:T(256)} %param.23) | copy-start | bytes 3076
  0.7 0.7 %copy-start.12 = (s32[256]{0:T(256)S(1)}, s32[256]{0:T(256)}, u32[]{:S(2)}) copy-start(s32[256]{0:T(256)} %param.24) | copy-start | bytes 3076
  0.7 0.7 %copy-start.9 = (s32[4,256]{1,0:T(4,128)S(1)}, s32[4,256]{1,0:T(4,128)}, u32[]{:S(2)}) copy-start(s32[4,256]{1,0:T(4,128)} %nbr_face.1) | copy-start | bytes 12292
  0.7 0.7 %copy-start.8 = (s32[4,256]{1,0:T(4,128)S(1)}, s32[4,256]{1,0:T(4,128)}, u32[]{:S(2)}) copy-start(s32[4,256]{1,0:T(4,128)} %nbr.1) | copy-start | bytes 12292
  0.7 0.7 %copy-start.10 = (s32[256]{0:T(256)S(1)}, s32[256]{0:T(256)}, u32[]{:S(2)}) copy-start(s32[256]{0:T(256)} %param.22) | copy-start | bytes 3076
  1.4 1.1 %copy-start = (f32[2,4,9,9,256]{4,1,3,2,0:T(4,128)S(1)}, f32[2,4,9,9,256]{4,1,3,2,0:T(4,128)}, u32[]{:S(2)}) copy-start(f32[2,4,9,9,256]{4,1,3,2,0:T(4,128)} %param.16) | copy-start | bytes 1990660
  2.5 1.0 %copy-start.1 = (f32[56,9,256]{2,0,1:T(8,128)S(1)}, f32[56,9,256]{2,0,1:T(8,128)}, u32[]{:S(2)}) copy-start(f32[56,9,256]{2,0,1:T(8,128)} %param.14) | copy-start | bytes 1548292
  3.5 1.0 %copy-start.2 = (f32[3,9,9,256]{3,0,2,1:T(4,128)S(1)}, f32[3,9,9,256]{3,0,2,1:T(4,128)}, u32[]{:S(2)}) copy-start(f32[3,9,9,256]{3,0,2,1:T(4,128)} %param.15) | copy-start | bytes 746500
  4.5 0.9 %copy-start.3 = (f32[3,56,56]{2,1,0:T(8,128)S(1)}, f32[3,56,56]{2,1,0:T(8,128)}, u32[]{:S(2)}) copy-start(f32[3,56,56]{2,1,0:T(8,128)} %stiff.1) | copy-start | bytes 112900
  5.4 0.9 %copy-start.4 = (f32[3,21,256]{2,1,0:T(8,128)S(1)}, f32[3,21,256]{2,1,0:T(8,128)}, u32[]{:S(2)}) copy-start(f32[3,21,256]{2,1,0:T(8,128)} %params.1) | copy-start | bytes 193540
  6.3 0.8 %copy-start.5 = (f32[4,21,56]{2,0,1:T(4,128)S(1)}, f32[4,21,56]{2,0,1:T(4,128)}, u32[]{:S(2)}) copy-start(f32[4,21,56]{2,0,1:T(4,128)} %param.18) | copy-start | bytes 56452
  7.1 0.8 %copy-start.6 = (f32[4,56,21]{1,0,2:T(4,128)S(1)}, f32[4,56,21]{1,0,2:T(4,128)}, u32[]{:S(2)}) copy-start(f32[4,56,21]{1,0,2:T(4,128)} %param.19) | copy-start | bytes 56452
  7.8 0.7 %copy-start.7 = (f32[21,256]{1,0:T(8,128)S(1)}, f32[21,256]{1,0:T(8,128)}, u32[]{:S(2)}) copy-start(f32[21,256]{1,0:T(8,128)} %state.1) | copy-start | bytes 64516

commit v2 on v1

--- a/solution.py
+++ b/solution.py
@@ -74,13 +74,16 @@
 
 
 def kernel(
-    dofs_h, star_h, flux_h, stiff, proj, lift, nbr, nbr_face, cluster, f_elem, f_face, f_target, params, state,
-    out_h, slip_out, state_out,
-    x, star, flux, st, wide, pad_sq, s4, st4, f4, l2, mem, own_of, etab, ubuf,
-    hsl, hsr, hrl, hrr, halo, amat, gmat, y, of, nb, fx, acc, pp,
+    dofs_h, star_h, flux_h, *rest
+):
+    small_h, rest = rest[:11], rest[11:]
+    (out_h, slip_h, state_h), rest = rest[:3], rest[3:]
+    small_v, rest = rest[:11], rest[11:]
+    stiff, proj, lift, nbr, nbr_face, cluster, f_elem, f_face, f_target, params, state = small_v
+    (slip_out, state_out, x, star, flux, st, wide, pad_sq, s4, st4, f4, f4b, l2, mem, own_of, etab,
+    hsl, hsr, hrl, hrr, amat, gmat, y, of, nb, fx, acc, pp,
     bq, mq, mq2, rq, bp, mp, mp2, rp, bs, ms, ms2, rs,
-    in_sem, out_sem, hs_sem, hr_sem, lo_s, lo_r, hi_s, hi_r,
-):
+    in_sem, out_sem, hs_sem, hr_sem, lo_s, lo_r, hi_s, hi_r) = rest
     me = lax.axis_index("dom")
     hi, lo = me // LO, me % LO
     n = LO * HI
@@ -91,7 +94,11 @@
         pltpu.make_async_copy(star_h, star, in_sem.at[1]),
         pltpu.make_async_copy(flux_h, flux, in_sem.at[2]),
     ]
-    for copy in in_copies:
+    small_copies = [
+        pltpu.make_async_copy(source, place, in_sem.at[3 + i])
+        for i, (source, place) in enumerate(zip(small_h, small_v))
+    ]
+    for copy in small_copies + in_copies:
         copy.start()
 
     barrier = pltpu.get_barrier_semaphore()
@@ -160,6 +167,8 @@
                 device_id=(right,), device_id_type=MESH),
         )
 
+    for copy in small_copies:
+        copy.wait()
     wide[...] = jnp.zeros_like(wide)
     for d in range(3):
         wide[d * B : (d + 1) * B, 0:B] = stiff[d]
@@ -173,6 +182,10 @@
     for f in range(NF):
         pad_sq[f * GP : f * GP + FB, 0:B] = proj[:, f, :]
     f4[...] = left_factor(pad_sq[...])
+    high, low = [jnp.concatenate([v, jnp.zeros((128, 128), F32)], axis=1) for v in split2(pad_sq[...])]
+    f4b[...] = (
+        high + pltpu.roll(high, B, axis=1) + pltpu.roll(low, 2 * B, axis=1) + pltpu.roll(low, 3 * B, axis=1)
+    ).astype(BF16)
     pad_sq[...] = jnp.zeros_like(pad_sq)
     for f in range(NF):
         pad_sq[f * GP : f * GP + FB, 0:B] = lift[:, f, :]
@@ -224,7 +237,7 @@
             st[q] = dot(left_w[...], stacked(source(q)))[0 : 3 * B]
             return 0
 
-        lax.fori_loop(0, Q, one, 0, unroll=3)
+        lax.fori_loop(0, Q, one, 0, unroll=True)
 
     def star_sum(store):
         def one(g, _):
@@ -252,18 +265,46 @@
 
     for copy in in_copies[:2]:
         copy.wait()
+    taylor(1)
     pl.semaphore_wait(barrier, LO + HI)
     send(lo_copy, LO, lo, bq, mq, HI, 0)
     pack_halo(0)
-    taylor(1)
     pack_halo(1)
+    taylor(2)
+    pack_halo(2)
+    taylor(3)
+    pack_halo(3)
 
     arrive(lo_copy, LO, bq, mq, HI, 0)
     for t in range(HI):
         mq2[t * LO : (t + 1) * LO, :] = mq[pl.ds(t, LO, stride=HI), :]
     send(hi_copy, HI, hi, mq2, rq, LO, 0)
-    taylor(2)
-    pack_halo(2)
+    taylor(4)
+    pack_halo(4)
+    taylor(5)
+    pack_halo(5)
+
+    level = cluster[...]
+
+    def by_level(values):
+        out = jnp.full((1, E), values[0], F32)
+        for c in range(1, NC):
+            out = jnp.where(level == c, values[c], out)
+        return out
+
+    step = by_level(TAUS)
+    own_w = [by_level([WEIGHTS[c][k] for c in range(NC)]) for k in range(ORD)]
+
+    def own_term(q, _):
+        total = own_w[0] * x[0, q]
+        for k in range(1, ORD):
+            total = total + own_w[k] * x[k, q]
+        wrapped = stacked(total)
+        st[q] = dot(st4[...], wrapped)[0 : 3 * B]
+        of[q] = dot(f4[...], wrapped)
+        return 0
+
+    lax.fori_loop(0, Q, own_term, 0, unroll=3)
 
     arrive(hi_copy, HI, mq2, rq, LO, 0)
     wanted = (iota((n, E), 1) + 1).astype(F32)
@@ -274,40 +315,6 @@
         for r in range(2):
             bp[t * 16 + r * LO : t * 16 + (r + 1) * LO, :] = answer[r * n + t * LO : r * n + (t + 1) * LO]
     send(hi_copy, HI, hi, bp, mp, 16, 1)
-    taylor(3)
-    pack_halo(3)
-
-    arrive(hi_copy, HI, bp, mp, 16, 1)
-    for t in range(LO):
-        for r in range(2):
-            mp2[t * 32 + r * HI : t * 32 + (r + 1) * HI, :] = mp[pl.ds(r * LO + t, HI, stride=16), :]
-    send(lo_copy, LO, lo, mp2, rp, 32, 1)
-    taylor(4)
-    pack_halo(4)
-    taylor(5)
-    pack_halo(5)
-
-    level = cluster[...]
-
-    def by_level(values):
-        out = jnp.full((1, E), values[0], F32)
-        for c in range(1, NC):
-            out = jnp.where(level == c, values[c], out)
-        return out
-
-    step = by_level(TAUS)
-    own_w = [by_level([WEIGHTS[c][k] for c in range(NC)]) for k in range(ORD)]
-
-    def own_term(q, _):
-        total = own_w[0] * x[0, q]
-        for k in range(1, ORD):
-            total = total + own_w[k] * x[k, q]
-        wrapped = stacked(total)
-        st[q] = dot(st4[...], wrapped)[0 : 3 * B]
-        of[q] = dot(f4[...], wrapped)
-        return 0
-
-    lax.fori_loop(0, Q, own_term, 0)
 
     def store_volume(p, lanes, value):
         acc[p, :, lanes] = x[0, p, :, lanes] + value
@@ -326,6 +333,29 @@
 
         lax.fori_loop(0, NC * EXT // E, build, 0)
 
+    def cluster_sums(terms, row, l):
+        for c in range(NC):
+            total = WEIGHTS[c][0] * terms[0]
+            for k in range(1, ORD):
+                total = total + WEIGHTS[c][k] * terms[k]
+            high, low = split2(total)
+            rows = pl.ds(pl.multiple_of(row * 2 * B, 16), 2 * B)
+            lanes = slice(c * EXT + l * 128, c * EXT + (l + 1) * 128)
+            amat[rows, lanes] = jnp.concatenate([high, low], axis=0).astype(BF16)
+
+    def own_integrals(q, _):
+        for l in range(2):
+            cluster_sums([x[k, q, :, l * 128 : (l + 1) * 128] for k in range(ORD)], q, l)
+        return 0
+
+    lax.fori_loop(0, Q, own_integrals, 0)
+
+    arrive(hi_copy, HI, bp, mp, 16, 1)
+    for t in range(LO):
+        for r in range(2):
+            mp2[t * 32 + r * HI : t * 32 + (r + 1) * HI, :] = mp[pl.ds(r * LO + t, HI, stride=16), :]
+    send(lo_copy, LO, lo, mp2, rp, 32, 1)
+
     keep_low = jnp.where(me > 0, 1, 0)
     keep_high = jnp.where(me < n - 1, 1, 0)
     keep = jnp.where(lane < RIM, keep_low, keep_high) > 0
@@ -333,49 +363,32 @@
         for copy in halo_copies(k):
             copy.wait_recv()
 
-        def unpack(q, _, k=k):
+    def rim_integrals(q, _):
+        first, second = [], []
+        for k in range(ORD):
             a, b = hrl[k, q], hrr[k, q]
-            first = jnp.where(low_half, a, pltpu.roll(b, RIM, axis=1))
-            halo[k, q] = jnp.where(keep, first, 0.0)
-            second = jnp.where(low_half, pltpu.roll(a, RIM, axis=1), b)
-            halo[k, q + 5] = jnp.where(keep, second, 0.0)
-            return 0
-
-        lax.fori_loop(0, 5, unpack, 0)
-
-    def integrals(q, _):
-        for l in range(3):
-            if l < 2:
-                terms = [x[k, q, :, l * 128 : (l + 1) * 128] for k in range(ORD)]
-            else:
-                terms = [halo[k, q] for k in range(ORD)]
-            for c in range(NC):
-                total = WEIGHTS[c][0] * terms[0]
-                for k in range(1, ORD):
-                    total = total + WEIGHTS[c][k] * terms[k]
-                high, low = split2(total)
-                rows = pl.ds(pl.multiple_of(q * 2 * B, 16), 2 * B)
-                lanes = slice(c * EXT + l * 128, c * EXT + (l + 1) * 128)
-                amat[rows, lanes] = jnp.concatenate([high, low], axis=0).astype(BF16)
+            first.append(jnp.where(keep, jnp.where(low_half, a, pltpu.roll(b, RIM, axis=1)), 0.0))
+            second.append(jnp.where(keep, jnp.where(low_half, pltpu.roll(a, RIM, axis=1), b), 0.0))
+        cluster_sums(first, q, 2)
+        cluster_sums(second, q + 5, 2)
         return 0
 
-    lax.fori_loop(0, Q, integrals, 0)
+    lax.fori_loop(0, 5, rim_integrals, 0)
 
     for f in range(NF):
-        y[...] = dot(amat[...], gmat[f])
+        y[...] = dot(amat[0 : Q * 2 * B, :], gmat[f]).astype(BF16)
         side = nbr_face[f : f + 1, :]
 
         def project(q, _, f=f, side=side):
-            base = pl.multiple_of(q * 2 * B, 8)
-            value = y[pl.ds(base, B), :] + y[pl.ds(base + B, B), :]
-            table = dot(f4[...], stacked(value))
+            half = y[pl.ds(pl.multiple_of(q * 2 * B, 16), 2 * B), :]
+            table = dot(f4b[...], jnp.concatenate([half, half, jnp.zeros((32, E), BF16)], axis=0))
             picked = table[0:24]
             for s in range(1, NF):
                 picked = jnp.where(side == s, table[s * GP : s * GP + 24], picked)
             nb[q, f * GP : f * GP + 24, :] = picked
             return 0
 
-        lax.fori_loop(0, Q, project, 0, unroll=3)
+        lax.fori_loop(0, Q, project, 0, unroll=True)
 
     arrive(lo_copy, LO, mp2, rp, 32, 1)
     by_slot = sum(dot(piece, mem[...]) for piece in split3(jnp.transpose(rp[...])))
@@ -411,6 +424,8 @@
         for piece in slips[f]:
             slot_slip = slot_slip + dot(piece, etab[f * E : (f + 1) * E, :])
     slip_out[...] = slot_slip[0:FB]
+    slip_copy = pltpu.make_async_copy(slip_out, slip_h, out_sem.at[1])
+    slip_copy.start()
     next_state = STEADY + (slot_state - STEADY) * jnp.exp(-jnp.abs(slot_slip))
     gap8, gap72 = jnp.zeros((8, E), F32), jnp.zeros((72, E), F32)
     wrapped = jnp.concatenate([next_state, gap8, next_state, gap72], axis=0)
@@ -449,8 +464,8 @@
         acc[p] = acc[p] - (surface[0:B] + surface[B : 2 * B])
         return 0
 
-    lax.fori_loop(0, Q, lifted, 0, unroll=3)
-    out_copy = pltpu.make_async_copy(acc, out_h, out_sem)
+    lax.fori_loop(0, Q, lifted, 0, unroll=True)
+    out_copy = pltpu.make_async_copy(acc, out_h, out_sem.at[0])
     out_copy.start()
 
     arrive(hi_copy, HI, ms2, rs, LO, 2)
@@ -459,6 +474,8 @@
     update = sum(dot(piece, own_of[...]) for piece in split3(news))
     hit = dot(jnp.ones((16, E), BF16), own_of[...])[0:1] > 0.5
     state_out[...] = jnp.where(hit, update[0:FB], state[...])
+    state_copy = pltpu.make_async_copy(state_out, state_h, out_sem.at[2])
+    state_copy.start()
 
     sent(lo_copy, LO, bq, mq, HI, 0)
     sent(hi_copy, HI, mq2, rq, LO, 0)
@@ -470,17 +487,20 @@
         for copy in halo_copies(k):
             copy.wait_send()
     out_copy.wait()
+    slip_copy.wait()
+    state_copy.wait()
 
 
 def local(*args):
     (elem_dofs, star_mats, flux_solver, stiffness, face_proj, lift_mats, neighbours, neighbour_face,
      cluster, fault_elem, fault_face, fault_target, fault_params, fault_state) = args
-    vmem, anywhere = pl.BlockSpec(memory_space=pltpu.VMEM), pl.BlockSpec(memory_space=pl.ANY)
+    anywhere = pl.BlockSpec(memory_space=pl.ANY)
     halo = pltpu.VMEM((ORD, 5, B, 128), F32)
     small = pltpu.VMEM((LO * HI, 128), F32)
     double = pltpu.VMEM((2 * LO * HI, 128), F32)
     faces = pltpu.VMEM((Q, NF * GP, E), F32)
     square = pltpu.VMEM((E, E), BF16)
+    row = pltpu.VMEM((1, E), I32)
     out, slip, state = pl.pallas_call(
         kernel,
         out_shape=(
@@ -488,9 +508,19 @@
             jax.ShapeDtypeStruct((FB, E), F32),
             jax.ShapeDtypeStruct((FB, E), F32),
         ),
-        in_specs=[anywhere] * 3 + [vmem] * 11,
-        out_specs=(anywhere, vmem, vmem),
+        in_specs=[anywhere] * 14,
+        out_specs=(anywhere,) * 3,
         scratch_shapes=[
+            pltpu.VMEM((3, B, B), F32),
+            pltpu.VMEM((FB, NF, B), F32),
+            pltpu.VMEM((FB, NF, B), F32),
+            pltpu.VMEM((NF, E), I32),
+            pltpu.VMEM((NF, E), I32),
+            row, row, row, row,
+            pltpu.VMEM((3, FB, E), F32),
+            pltpu.VMEM((FB, E), F32),
+            pltpu.VMEM((FB, E), F32),
+            pltpu.VMEM((FB, E), F32),
             pltpu.VMEM((ORD, Q, B, E), F32),
             pltpu.VMEM((Q, Q, 3, E), F32),
             pltpu.VMEM((2, Q, Q, NF, E), F32),
@@ -500,24 +530,23 @@
             pltpu.VMEM((176, 256), BF16),
             pltpu.VMEM((176, 256), BF16),
             pltpu.VMEM((128, 256), BF16),
+            pltpu.VMEM((128, 256), BF16),
             pltpu.VMEM((112, 256), BF16),
             square,
             square,
             pltpu.VMEM((NF * E, E), BF16),
-            pltpu.VMEM((8, 128), F32),
             halo, halo, halo, halo,
-            pltpu.VMEM((ORD, 10, B, 128), F32),
-            pltpu.VMEM((Q * 2 * B, NC * EXT), BF16),
+            pltpu.VMEM((10 * 2 * B, NC * EXT), BF16),
             pltpu.VMEM((NF, NC * EXT, E), BF16),
-            pltpu.VMEM((Q * 2 * B, E), F32),
+            pltpu.VMEM((Q * 2 * B, E), BF16),
             faces, faces, faces,
             pltpu.VMEM((Q, B, E), F32),
             pltpu.VMEM((128, E), F32),
             small, small, small, small,
             double, double, double, double,
             small, small, small, small,
+            pltpu.SemaphoreType.DMA((14,)),
             pltpu.SemaphoreType.DMA((3,)),
-            pltpu.SemaphoreType.DMA,
             pltpu.SemaphoreType.DMA((2, ORD)),
             pltpu.SemaphoreType.DMA((2, ORD)),
             pltpu.SemaphoreType.DMA((3, LO)),
@@ -526,7 +555,7 @@
             pltpu.SemaphoreType.DMA((3, HI)),
         ],
         compiler_params=pltpu.CompilerParams(
-            collective_id=0, has_side_effects=True, vmem_limit_bytes=48 * 1024 * 1024
+            collective_id=0, has_side_effects=True, vmem_limit_bytes=60 * 1024 * 1024
         ),
     )(
         jnp.transpose(elem_dofs, (1, 0, 2)),

time: 66.1 us -> 54.3 us (0.82)
  local copies, waits for them, and re-layouts: 9.89 us -> 3.23 us
  Pallas kernels: 55 us -> 50.2 us
    unnamed x31 -> x7, local copies, waits for them, and re-layouts: 9.89 us -> 3.23 us
    pallas_call x1, Pallas kernels: 55 us -> 50.2 us  [local(): pl.pallas_call(kernel, out_shape=(jax.ShapeDtypeStruct((Q, B, E), F32), j...]
where the time goes in v2:
time: 54.3 us; the launch traced here: 54.1 us
  Pallas kernels  50.2 us (92%)
  local copies, waits for them, and re-layouts  3.23 us (6%)
  between operations  0.65 us (1%)
    pallas_call x1, Pallas kernels, local(): pl.pallas_call(kernel, out_shape=(jax.ShapeDtypeStruct((Q, B, E), F32), j...  50.2 us
    unnamed x7, local copies, waits for them, and re-layouts  3.23 us

profile of v2, /device:TPU:1, one launch (start us, length us, event | category | flops | bytes accessed | tf_op | source)
XLA Modules:
  0.0 54.1 jit_solution(13099184073281106754)
XLA Ops:
  0.6 50.2 %shard_map.157 = (f32[9,56,256]{2,1,0:T(8,128)}, f32[21,256]{1,0:T(8,128)}, f32[21,256]{1,0:T(8,128)}) custom-call(f32[9,56,256]{2,1,0:T(8,128)} %bitcast.11, f32[9,9,3,256]{3,2,1,0:T(4,128)} %bitcast.13, f32[2,9,9,4,256]{4,3,2,1,0:T(4,128)} %bitcast.10, f32[3,56,56]{2,1,0:T(8,128)} %rest_0_.1, f32[21,4,56]{2,1,0:T(4,128)} %bitcast.14, ...), custom_call_target="tpu_custom_call" | custom-call | tf_op jit(solution)/shard_map/pallas_call | solution.py:504
  50.9 0.0 copy-start.1
  50.9 1.9 %copy.20 = f32[56,9,256]{2,0,1:T(8,128)} copy(f32[56,9,256]{2,0,1:T(8,128)} %bitcast.12) | data formatting | bytes 1032192
  52.7 0.0 copy-done.1
  52.7 0.0 copy-start
  52.7 0.6 %copy.21 = f32[21,256]{1,0:T(8,128)} copy(f32[21,256]{1,0:T(8,128)S(1)} %copy-done.1) | data formatting | bytes 43008
  53.4 0.1 copy-done
  53.5 0.6 %copy.22 = f32[21,256]{1,0:T(8,128)} copy(f32[21,256]{1,0:T(8,128)S(1)} %copy-done) | data formatting | bytes 43008
Async XLA Ops:
  50.9 1.9 %copy-start.1 = (f32[21,256]{1,0:T(8,128)S(1)}, f32[21,256]{1,0:T(8,128)}, u32[]{:S(2)}) copy-start(f32[21,256]{1,0:T(8,128)} %get-tuple-element.13) | copy-start | bytes 64516
  52.7 0.7 %copy-start = (f32[21,256]{1,0:T(8,128)S(1)}, f32[21,256]{1,0:T(8,128)}, u32[]{:S(2)}) copy-start(f32[21,256]{1,0:T(8,128)} %get-tuple-element.14) | copy-start | bytes 64516

commit v3 on v2

--- a/solution.py
+++ b/solution.py
@@ -11,7 +11,9 @@
 MESH = pl.DeviceIdType.MESH
 B, Q, FB, ORD, NF, NC, NEWTON = 56, 9, 21, 6, 4, 4, 4
 E, RIM = 256, 64
-LO, HI = 8, 16
+N = 128
+ORDER = (0, 3, 7, 1, 2, 4, 5, 6, 8)
+FIRST = 3 * 2 * B
 GP = 32
 EXT = 384
 BASE_STEP, STEADY = 0.2, 0.8
@@ -77,16 +79,15 @@
     dofs_h, star_h, flux_h, *rest
 ):
     small_h, rest = rest[:11], rest[11:]
-    (out_h, slip_h, state_h), rest = rest[:3], rest[3:]
+    (acc, slip_out, state_out), rest = rest[:3], rest[3:]
     small_v, rest = rest[:11], rest[11:]
     stiff, proj, lift, nbr, nbr_face, cluster, f_elem, f_face, f_target, params, state = small_v
-    (slip_out, state_out, x, star, flux, st, wide, pad_sq, s4, st4, f4, f4b, l2, mem, own_of, etab,
-    hsl, hsr, hrl, hrr, amat, gmat, y, of, nb, fx, acc, pp,
-    bq, mq, mq2, rq, bp, mp, mp2, rp, bs, ms, ms2, rs,
-    in_sem, out_sem, hs_sem, hr_sem, lo_s, lo_r, hi_s, hi_r) = rest
+    (x, star, flux, st, wide, pad_sq, s4, st4, f4, f4b, l2, mem, own_of, etab,
+    hsl, hsr, hrl, hrr, amat, gmat, y, of, nb, fx, pp,
+    bq, rq, bp, rp, bs, rs,
+    in_sem, hs_sem, hr_sem, ex_s, ex_r, ex_o) = rest
     me = lax.axis_index("dom")
-    hi, lo = me // LO, me % LO
-    n = LO * HI
+    n = N
     left, right = (me + n - 1) % n, (me + 1) % n
 
     in_copies = [
@@ -103,59 +104,39 @@
 
     barrier = pltpu.get_barrier_semaphore()
 
-    def greet_lo(j, _):
-        pl.semaphore_signal(barrier, inc=1, device_id=(hi * LO + (lo + j) % LO,), device_id_type=MESH)
+    def greet(j, _):
+        pl.semaphore_signal(barrier, inc=1, device_id=((me + j) % n,), device_id_type=MESH)
         return 0
 
-    def greet_hi(j, _):
-        pl.semaphore_signal(barrier, inc=1, device_id=(((hi + j) % HI) * LO + lo,), device_id_type=MESH)
-        return 0
-
-    lax.fori_loop(1, LO, greet_lo, 0)
-    lax.fori_loop(1, HI, greet_hi, 0)
-    pl.semaphore_signal(barrier, inc=1, device_id=(left,), device_id_type=MESH)
-    pl.semaphore_signal(barrier, inc=1, device_id=(right,), device_id_type=MESH)
-
-    def lo_copy(buf, dst, rows, which, j):
-        t = (lo + j) % LO
+    lax.fori_loop(1, n, greet, 0)
+
+    def row_copy(buf, dst, rows, which, j):
+        t = (me + j) % n
         return pltpu.make_async_remote_copy(
-            src_ref=buf.at[pl.ds(pl.multiple_of(t * rows, 8), rows)],
-            dst_ref=dst.at[pl.ds(pl.multiple_of(lo * rows, 8), rows)],
-            send_sem=lo_s.at[which, j], recv_sem=lo_r.at[which, j],
-            device_id=(hi * LO + t,), device_id_type=MESH,
+            src_ref=buf.at[pl.ds(t * rows, rows)],
+            dst_ref=dst.at[pl.ds(me * rows, rows)],
+            send_sem=ex_s.at[which], recv_sem=ex_r.at[which],
+            device_id=(t,), device_id_type=MESH,
         )
 
-    def hi_copy(buf, dst, rows, which, j):
-        t = (hi + j) % HI
-        return pltpu.make_async_remote_copy(
-            src_ref=buf.at[pl.ds(pl.multiple_of(t * rows, 8), rows)],
-            dst_ref=dst.at[pl.ds(pl.multiple_of(hi * rows, 8), rows)],
-            send_sem=hi_s.at[which, j], recv_sem=hi_r.at[which, j],
-            device_id=(t * LO + lo,), device_id_type=MESH,
-        )
-
-    def send(make, count, mine, buf, dst, rows, which):
+    def send(buf, dst, rows, which):
         def one(j, _):
-            make(buf, dst, rows, which, j).start()
+            row_copy(buf, dst, rows, which, j).start()
             return 0
 
-        lax.fori_loop(1, count, one, 0)
-        block = pl.ds(pl.multiple_of(mine * rows, 8), rows)
-        dst[block, :] = buf[block, :]
-
-    def arrive(make, count, buf, dst, rows, which):
-        def one(j, _):
-            make(buf, dst, rows, which, j).wait_recv()
-            return 0
-
-        lax.fori_loop(1, count, one, 0)
-
-    def sent(make, count, buf, dst, rows, which):
-        def one(j, _):
-            make(buf, dst, rows, which, j).wait_send()
-            return 0
-
-        lax.fori_loop(1, count, one, 0)
+        lax.fori_loop(1, n, one, 0)
+        pltpu.make_async_copy(buf.at[pl.ds(me * rows, rows)], dst.at[pl.ds(me * rows, rows)], ex_o.at[which]).start()
+
+    def arrive(buf, dst, rows, which):
+        pltpu.make_async_copy(buf.at[pl.ds(me * rows, rows)], dst.at[pl.ds(me * rows, rows)], ex_o.at[which]).wait()
+        pltpu.make_async_copy(
+            buf.at[pl.ds(0, (n - 1) * rows)], dst.at[pl.ds(0, (n - 1) * rows)], ex_r.at[which]
+        ).wait()
+
+    def sent(buf, dst, rows, which):
+        pltpu.make_async_copy(
+            buf.at[pl.ds(0, (n - 1) * rows)], dst.at[pl.ds(0, (n - 1) * rows)], ex_s.at[which]
+        ).wait()
 
     def halo_copies(k):
         return (
@@ -182,7 +163,10 @@
     for f in range(NF):
         pad_sq[f * GP : f * GP + FB, 0:B] = proj[:, f, :]
     f4[...] = left_factor(pad_sq[...])
-    high, low = [jnp.concatenate([v, jnp.zeros((128, 128), F32)], axis=1) for v in split2(pad_sq[...])]
+    pad_sq[...] = jnp.zeros_like(pad_sq)
+    for f in range(NF):
+        pad_sq[f * 24 : f * 24 + FB, 0:B] = proj[:, f, :]
+    high, low = [jnp.concatenate([v, jnp.zeros((96, 128), F32)], axis=1) for v in split2(pad_sq[0:96, :])]
     f4b[...] = (
         high + pltpu.roll(high, B, axis=1) + pltpu.roll(low, 2 * B, axis=1) + pltpu.roll(low, 3 * B, axis=1)
     ).astype(BF16)
@@ -206,29 +190,25 @@
     earlier = jnp.where(iota((E, E), 0) < iota((E, E), 1), 1.0, 0.0).astype(BF16)
     before = dot(member.astype(BF16), earlier)
     rank = jnp.sum(member * before, axis=0, keepdims=True)
-    place = (jnp.bitwise_and(owner, LO - 1) * (2 * HI) + lax.shift_right_logical(owner, 3)).astype(F32) + HI * rank
+    place = owner.astype(F32) + n * rank
     place = jnp.where(live, place, -1.0)
     mem[...] = jnp.where(iota((E, E), 0).astype(F32) == place, 1.0, 0.0).astype(BF16)
     grid_place = jnp.where(live, f_face[...] * E + f_elem[...], -1)
     for f in range(NF):
         etab[f * E : (f + 1) * E, :] = jnp.where(iota((E, E), 0) + f * E == grid_place, 1.0, 0.0).astype(BF16)
     ids = jnp.where(iota((128, E), 0) < 2, (slot + 1).astype(F32), 0.0).astype(BF16)
-    asked = dot_nt(mem[...], ids).reshape(LO, 2, HI, 128)
-    lane3 = iota((LO, HI, 128), 2)
-    bq[...] = jnp.where(lane3 == 0, asked[:, 0], asked[:, 1]).reshape(n, 128)
+    asked = dot_nt(mem[...], ids)
+    lane2 = iota((n, 128), 1)
+    bq[...] = jnp.where(lane2 == 0, asked[0:n], asked[n : 2 * n])
 
     lane = iota((B, 128), 1)
     low_half = lane < RIM
 
     def pack_halo(k):
-        def one(q, _):
-            a, b = x[k, q, :, 0:128], x[k, jnp.minimum(q + 5, Q - 1), :, 0:128]
-            hsl[k, q] = jnp.where(low_half, a, pltpu.roll(b, RIM, axis=1))
-            a, b = x[k, q, :, 128:256], x[k, jnp.minimum(q + 5, Q - 1), :, 128:256]
-            hsr[k, q] = jnp.where(low_half, pltpu.roll(a, RIM, axis=1), b)
-            return 0
-
-        lax.fori_loop(0, 5, one, 0)
+        for q in range(5):
+            r = min(q + 5, Q - 1)
+            hsl[k, q] = jnp.where(low_half, x[k, q, :, 0:128], pltpu.roll(x[k, r, :, 0:128], RIM, axis=1))
+            hsr[k, q] = jnp.where(low_half, pltpu.roll(x[k, q, :, 128:256], RIM, axis=1), x[k, r, :, 128:256])
         for copy in halo_copies(k):
             copy.start()
 
@@ -266,23 +246,22 @@
     for copy in in_copies[:2]:
         copy.wait()
     taylor(1)
-    pl.semaphore_wait(barrier, LO + HI)
-    send(lo_copy, LO, lo, bq, mq, HI, 0)
+    pl.semaphore_wait(barrier, n - 1)
     pack_halo(0)
     pack_halo(1)
-    taylor(2)
-    pack_halo(2)
-    taylor(3)
-    pack_halo(3)
-
-    arrive(lo_copy, LO, bq, mq, HI, 0)
-    for t in range(HI):
-        mq2[t * LO : (t + 1) * LO, :] = mq[pl.ds(t, LO, stride=HI), :]
-    send(hi_copy, HI, hi, mq2, rq, LO, 0)
-    taylor(4)
-    pack_halo(4)
-    taylor(5)
-    pack_halo(5)
+    send(bq, rq, 1, 0)
+    for k in range(2, ORD):
+        taylor(k)
+        pack_halo(k)
+
+    arrive(bq, rq, 1, 0)
+    wanted = (iota((n, E), 1) + 1).astype(F32)
+    for r in range(2):
+        own_of[r * n : (r + 1) * n, :] = jnp.where(rq[:, r : r + 1] == wanted, 1.0, 0.0).astype(BF16)
+    answer = sum(dot_nt(own_of[...], piece) for piece in split3(pp[...]))
+    for r in range(2):
+        bp[pl.ds(r, n, stride=2), :] = answer[r * n : (r + 1) * n]
+    send(bp, rp, 2, 1)
 
     level = cluster[...]
 
@@ -306,21 +285,6 @@
 
     lax.fori_loop(0, Q, own_term, 0, unroll=3)
 
-    arrive(hi_copy, HI, mq2, rq, LO, 0)
-    wanted = (iota((n, E), 1) + 1).astype(F32)
-    for r in range(2):
-        own_of[r * n : (r + 1) * n, :] = jnp.where(rq[:, r : r + 1] == wanted, 1.0, 0.0).astype(BF16)
-    answer = sum(dot_nt(own_of[...], piece) for piece in split3(pp[...]))
-    for t in range(HI):
-        for r in range(2):
-            bp[t * 16 + r * LO : t * 16 + (r + 1) * LO, :] = answer[r * n + t * LO : r * n + (t + 1) * LO]
-    send(hi_copy, HI, hi, bp, mp, 16, 1)
-
-    def store_volume(p, lanes, value):
-        acc[p, :, lanes] = x[0, p, :, lanes] + value
-
-    star_sum(store_volume)
-
     number = nbr[...] - me * E
     ext = jnp.where(number < RIM, number + E, jnp.where(number >= E + RIM, number, number - RIM))
     column = level * EXT + ext
@@ -339,22 +303,13 @@
             for k in range(1, ORD):
                 total = total + WEIGHTS[c][k] * terms[k]
             high, low = split2(total)
-            rows = pl.ds(pl.multiple_of(row * 2 * B, 16), 2 * B)
+            rows = slice(row * 2 * B, (row + 1) * 2 * B)
             lanes = slice(c * EXT + l * 128, c * EXT + (l + 1) * 128)
             amat[rows, lanes] = jnp.concatenate([high, low], axis=0).astype(BF16)
 
-    def own_integrals(q, _):
+    for q in range(Q):
         for l in range(2):
-            cluster_sums([x[k, q, :, l * 128 : (l + 1) * 128] for k in range(ORD)], q, l)
-        return 0
-
-    lax.fori_loop(0, Q, own_integrals, 0)
-
-    arrive(hi_copy, HI, bp, mp, 16, 1)
-    for t in range(LO):
-        for r in range(2):
-            mp2[t * 32 + r * HI : t * 32 + (r + 1) * HI, :] = mp[pl.ds(r * LO + t, HI, stride=16), :]
-    send(lo_copy, LO, lo, mp2, rp, 32, 1)
+            cluster_sums([x[k, q, :, l * 128 : (l + 1) * 128] for k in range(ORD)], ORDER.index(q), l)
 
     keep_low = jnp.where(me > 0, 1, 0)
     keep_high = jnp.where(me < n - 1, 1, 0)
@@ -363,35 +318,42 @@
         for copy in halo_copies(k):
             copy.wait_recv()
 
-    def rim_integrals(q, _):
+    for q in range(5):
         first, second = [], []
         for k in range(ORD):
             a, b = hrl[k, q], hrr[k, q]
             first.append(jnp.where(keep, jnp.where(low_half, a, pltpu.roll(b, RIM, axis=1)), 0.0))
-            second.append(jnp.where(keep, jnp.where(low_half, pltpu.roll(a, RIM, axis=1), b), 0.0))
-        cluster_sums(first, q, 2)
-        cluster_sums(second, q + 5, 2)
-        return 0
-
-    lax.fori_loop(0, 5, rim_integrals, 0)
-
-    for f in range(NF):
-        y[...] = dot(amat[0 : Q * 2 * B, :], gmat[f]).astype(BF16)
-        side = nbr_face[f : f + 1, :]
-
-        def project(q, _, f=f, side=side):
-            half = y[pl.ds(pl.multiple_of(q * 2 * B, 16), 2 * B), :]
+            if q + 5 < Q:
+                second.append(jnp.where(keep, jnp.where(low_half, pltpu.roll(a, RIM, axis=1), b), 0.0))
+        cluster_sums(first, ORDER.index(q), 2)
+        if q + 5 < Q:
+            cluster_sums(second, ORDER.index(q + 5), 2)
+
+    def gather(start, stop):
+        def one(f, _):
+            y[f, start:stop, :] = dot(amat[start:stop, :], gmat[f]).astype(BF16)
+            return 0
+
+        lax.fori_loop(0, NF, one, 0)
+
+    def project(q):
+        start = ORDER.index(q) * 2 * B
+        for f in range(NF):
+            side = nbr_face[f : f + 1, :]
+            half = y[f, start : start + 2 * B, :]
             table = dot(f4b[...], jnp.concatenate([half, half, jnp.zeros((32, E), BF16)], axis=0))
             picked = table[0:24]
             for s in range(1, NF):
-                picked = jnp.where(side == s, table[s * GP : s * GP + 24], picked)
+                picked = jnp.where(side == s, table[s * 24 : (s + 1) * 24], picked)
             nb[q, f * GP : f * GP + 24, :] = picked
-            return 0
-
-        lax.fori_loop(0, Q, project, 0, unroll=True)
-
-    arrive(lo_copy, LO, mp2, rp, 32, 1)
-    by_slot = sum(dot(piece, mem[...]) for piece in split3(jnp.transpose(rp[...])))
+
+    gather(0, FIRST)
+    for q in ORDER[:3]:
+        project(q)
+
+    arrive(bp, rp, 2, 1)
+    given = jnp.concatenate([rp[pl.ds(r, n, stride=2), :] for r in range(2)], axis=0)
+    by_slot = sum(dot(piece, mem[...]) for piece in split3(jnp.transpose(given)))
     by_slot = jnp.where(iota((128, E), 0) == 96, 1.0, by_slot)
     slot_state = by_slot[72:96]
     slot_pieces = split3(by_slot)
@@ -424,14 +386,21 @@
         for piece in slips[f]:
             slot_slip = slot_slip + dot(piece, etab[f * E : (f + 1) * E, :])
     slip_out[...] = slot_slip[0:FB]
-    slip_copy = pltpu.make_async_copy(slip_out, slip_h, out_sem.at[1])
-    slip_copy.start()
     next_state = STEADY + (slot_state - STEADY) * jnp.exp(-jnp.abs(slot_slip))
     gap8, gap72 = jnp.zeros((8, E), F32), jnp.zeros((72, E), F32)
     wrapped = jnp.concatenate([next_state, gap8, next_state, gap72], axis=0)
-    told = sum(dot_nt(mem[...], piece) for piece in split3(wrapped)).reshape(LO, 2, HI, 128)
-    bs[...] = jnp.where(lane3 < 32, told[:, 0], told[:, 1]).reshape(n, 128)
-    send(lo_copy, LO, lo, bs, ms, HI, 2)
+    told = sum(dot_nt(mem[...], piece) for piece in split3(wrapped))
+    bs[...] = jnp.where(lane2 < 32, told[0:n], told[n : 2 * n])
+    send(bs, rs, 1, 2)
+
+    gather(FIRST, Q * 2 * B)
+    for q in ORDER[3:]:
+        project(q)
+
+    def store_volume(p, lanes, value):
+        acc[p, :, lanes] = x[0, p, :, lanes] + value
+
+    star_sum(store_volume)
 
     in_copies[2].wait()
 
@@ -452,11 +421,6 @@
 
     lax.fori_loop(0, 3, fluxes, 0)
 
-    arrive(lo_copy, LO, bs, ms, HI, 2)
-    for t in range(HI):
-        ms2[t * LO : (t + 1) * LO, :] = ms[pl.ds(t, LO, stride=HI), :]
-    send(hi_copy, HI, hi, ms2, rs, LO, 2)
-
     def lifted(p, _):
         high, low = split2(fx[p])
         both = jnp.concatenate([high, low], axis=0).astype(BF16)
@@ -465,39 +429,28 @@
         return 0
 
     lax.fori_loop(0, Q, lifted, 0, unroll=True)
-    out_copy = pltpu.make_async_copy(acc, out_h, out_sem.at[0])
-    out_copy.start()
-
-    arrive(hi_copy, HI, ms2, rs, LO, 2)
+    arrive(bs, rs, 1, 2)
     turned = jnp.transpose(rs[...])
     news = jnp.concatenate([turned[0:24], turned[32:56]], axis=1)
     update = sum(dot(piece, own_of[...]) for piece in split3(news))
     hit = dot(jnp.ones((16, E), BF16), own_of[...])[0:1] > 0.5
     state_out[...] = jnp.where(hit, update[0:FB], state[...])
-    state_copy = pltpu.make_async_copy(state_out, state_h, out_sem.at[2])
-    state_copy.start()
-
-    sent(lo_copy, LO, bq, mq, HI, 0)
-    sent(hi_copy, HI, mq2, rq, LO, 0)
-    sent(hi_copy, HI, bp, mp, 16, 1)
-    sent(lo_copy, LO, mp2, rp, 32, 1)
-    sent(lo_copy, LO, bs, ms, HI, 2)
-    sent(hi_copy, HI, ms2, rs, LO, 2)
+
+    sent(bq, rq, 1, 0)
+    sent(bp, rp, 2, 1)
+    sent(bs, rs, 1, 2)
     for k in range(ORD):
         for copy in halo_copies(k):
             copy.wait_send()
-    out_copy.wait()
-    slip_copy.wait()
-    state_copy.wait()
 
 
 def local(*args):
     (elem_dofs, star_mats, flux_solver, stiffness, face_proj, lift_mats, neighbours, neighbour_face,
      cluster, fault_elem, fault_face, fault_target, fault_params, fault_state) = args
-    anywhere = pl.BlockSpec(memory_space=pl.ANY)
+    vmem, hbm = pl.BlockSpec(memory_space=pltpu.VMEM), pl.BlockSpec(memory_space=pl.ANY)
     halo = pltpu.VMEM((ORD, 5, B, 128), F32)
-    small = pltpu.VMEM((LO * HI, 128), F32)
-    double = pltpu.VMEM((2 * LO * HI, 128), F32)
+    small = pltpu.VMEM((N, 128), F32)
+    double = pltpu.VMEM((2 * N, 128), F32)
     faces = pltpu.VMEM((Q, NF * GP, E), F32)
     square = pltpu.VMEM((E, E), BF16)
     row = pltpu.VMEM((1, E), I32)
@@ -508,8 +461,8 @@
             jax.ShapeDtypeStruct((FB, E), F32),
             jax.ShapeDtypeStruct((FB, E), F32),
         ),
-        in_specs=[anywhere] * 14,
-        out_specs=(anywhere,) * 3,
+        in_specs=[hbm] * 14,
+        out_specs=(vmem,) * 3,
         scratch_shapes=[
             pltpu.VMEM((3, B, B), F32),
             pltpu.VMEM((FB, NF, B), F32),
@@ -518,8 +471,6 @@
             pltpu.VMEM((NF, E), I32),
             row, row, row, row,
             pltpu.VMEM((3, FB, E), F32),
-            pltpu.VMEM((FB, E), F32),
-            pltpu.VMEM((FB, E), F32),
             pltpu.VMEM((FB, E), F32),
             pltpu.VMEM((ORD, Q, B, E), F32),
             pltpu.VMEM((Q, Q, 3, E), F32),
@@ -530,29 +481,24 @@
             pltpu.VMEM((176, 256), BF16),
             pltpu.VMEM((176, 256), BF16),
             pltpu.VMEM((128, 256), BF16),
-            pltpu.VMEM((128, 256), BF16),
+            pltpu.VMEM((96, 256), BF16),
             pltpu.VMEM((112, 256), BF16),
             square,
             square,
             pltpu.VMEM((NF * E, E), BF16),
             halo, halo, halo, halo,
-            pltpu.VMEM((10 * 2 * B, NC * EXT), BF16),
+            pltpu.VMEM((Q * 2 * B, NC * EXT), BF16),
             pltpu.VMEM((NF, NC * EXT, E), BF16),
-            pltpu.VMEM((Q * 2 * B, E), BF16),
+            pltpu.VMEM((NF, Q * 2 * B, E), BF16),
             faces, faces, faces,
-            pltpu.VMEM((Q, B, E), F32),
             pltpu.VMEM((128, E), F32),
-            small, small, small, small,
-            double, double, double, double,
-            small, small, small, small,
+            small, small, double, double, small, small,
             pltpu.SemaphoreType.DMA((14,)),
-            pltpu.SemaphoreType.DMA((3,)),
             pltpu.SemaphoreType.DMA((2, ORD)),
             pltpu.SemaphoreType.DMA((2, ORD)),
-            pltpu.SemaphoreType.DMA((3, LO)),
-            pltpu.SemaphoreType.DMA((3, LO)),
-            pltpu.SemaphoreType.DMA((3, HI)),
-            pltpu.SemaphoreType.DMA((3, HI)),
+            pltpu.SemaphoreType.DMA((3,)),
+            pltpu.SemaphoreType.DMA((3,)),
+            pltpu.SemaphoreType.DMA((3,)),
         ],
         compiler_params=pltpu.CompilerParams(
             collective_id=0, has_side_effects=True, vmem_limit_bytes=60 * 1024 * 1024

time: 54.3 us -> 42.6 us (0.78)
  Pallas kernels: 50.2 us -> 38.5 us
    pallas_call x1, Pallas kernels: 50.2 us -> 38.5 us  [local(): pl.pallas_call(kernel, out_shape=(jax.ShapeDtypeStruct((Q, B, E), F32), j...]
where the time goes in v3:
time: 42.6 us; the launch traced here: 42.4 us
  Pallas kernels  38.5 us (90%)
  local copies, waits for them, and re-layouts  3.23 us (8%)
  between operations  0.65 us (2%)
    pallas_call x1, Pallas kernels, local(): pl.pallas_call(kernel, out_shape=(jax.ShapeDtypeStruct((Q, B, E), F32), j...  38.5 us
    unnamed x7, local copies, waits for them, and re-layouts  3.23 us

profile of v3, /device:TPU:1, one launch (start us, length us, event | category | flops | bytes accessed | tf_op | source)
XLA Modules:
  0.0 42.4 jit_solution(11120016606347216508)
XLA Ops:
  0.6 38.5 %shard_map.157 = (f32[9,56,256]{2,1,0:T(8,128)}, f32[21,256]{1,0:T(8,128)}, f32[21,256]{1,0:T(8,128)}) custom-call(f32[9,56,256]{2,1,0:T(8,128)} %bitcast.11, f32[9,9,3,256]{3,2,1,0:T(4,128)} %bitcast.13, f32[2,9,9,4,256]{4,3,2,1,0:T(4,128)} %bitcast.10, f32[3,56,56]{2,1,0:T(8,128)} %rest_0_.1, f32[21,4,56]{2,1,0:T(4,128)} %bitcast.14, ...), custom_call_target="tpu_custom_call" | custom-call | tf_op jit(solution)/shard_map/pallas_call | solution.py:457
  39.1 0.0 copy-start.1
  39.1 1.9 %copy.20 = f32[56,9,256]{2,0,1:T(8,128)} copy(f32[56,9,256]{2,0,1:T(8,128)} %bitcast.12) | data formatting | bytes 1032192
  41.0 0.0 copy-done.1
  41.0 0.0 copy-start
  41.0 0.6 %copy.21 = f32[21,256]{1,0:T(8,128)} copy(f32[21,256]{1,0:T(8,128)S(1)} %copy-done.1) | data formatting | bytes 43008
  41.6 0.1 copy-done
  41.8 0.6 %copy.22 = f32[21,256]{1,0:T(8,128)} copy(f32[21,256]{1,0:T(8,128)S(1)} %copy-done) | data formatting | bytes 43008
Async XLA Ops:
  39.1 1.9 %copy-start.1 = (f32[21,256]{1,0:T(8,128)S(1)}, f32[21,256]{1,0:T(8,128)}, u32[]{:S(2)}) copy-start(f32[21,256]{1,0:T(8,128)} %get-tuple-element.13) | copy-start | bytes 64516
  41.0 0.7 %copy-start = (f32[21,256]{1,0:T(8,128)S(1)}, f32[21,256]{1,0:T(8,128)}, u32[]{:S(2)}) copy-start(f32[21,256]{1,0:T(8,128)} %get-tuple-element.14) | copy-start | bytes 64516

commit v4 on v3

--- a/solution.py
+++ b/solution.py
@@ -104,14 +104,17 @@
 
     barrier = pltpu.get_barrier_semaphore()
 
-    def greet(j, _):
-        pl.semaphore_signal(barrier, inc=1, device_id=((me + j) % n,), device_id_type=MESH)
-        return 0
-
-    lax.fori_loop(1, n, greet, 0)
-
-    def row_copy(buf, dst, rows, which, j):
-        t = (me + j) % n
+    def others(action):
+        def one(t, _):
+            action(t)
+            return 0
+
+        lax.fori_loop(me + 1, n, one, 0)
+        lax.fori_loop(0, me, one, 0)
+
+    others(lambda t: pl.semaphore_signal(barrier, inc=1, device_id=(t,), device_id_type=MESH))
+
+    def row_copy(buf, dst, rows, which, t):
         return pltpu.make_async_remote_copy(
             src_ref=buf.at[pl.ds(t * rows, rows)],
             dst_ref=dst.at[pl.ds(me * rows, rows)],
@@ -120,11 +123,7 @@
         )
 
     def send(buf, dst, rows, which):
-        def one(j, _):
-            row_copy(buf, dst, rows, which, j).start()
-            return 0
-
-        lax.fori_loop(1, n, one, 0)
+        others(lambda t: row_copy(buf, dst, rows, which, t).start())
         pltpu.make_async_copy(buf.at[pl.ds(me * rows, rows)], dst.at[pl.ds(me * rows, rows)], ex_o.at[which]).start()
 
     def arrive(buf, dst, rows, which):
@@ -201,14 +200,16 @@
     lane2 = iota((n, 128), 1)
     bq[...] = jnp.where(lane2 == 0, asked[0:n], asked[n : 2 * n])
 
-    lane = iota((B, 128), 1)
+    lane = iota((32, 128), 1)
     low_half = lane < RIM
 
-    def pack_halo(k):
-        for q in range(5):
-            r = min(q + 5, Q - 1)
-            hsl[k, q] = jnp.where(low_half, x[k, q, :, 0:128], pltpu.roll(x[k, r, :, 0:128], RIM, axis=1))
-            hsr[k, q] = jnp.where(low_half, pltpu.roll(x[k, q, :, 128:256], RIM, axis=1), x[k, r, :, 128:256])
+    def pack_halo(k, q, half, value):
+        if half == 0:
+            hsl[k, q] = jnp.where(low_half, value[0:32], pltpu.roll(value[24:56], RIM, axis=1))
+        else:
+            hsr[k, q] = jnp.where(low_half, pltpu.roll(value[0:32], RIM, axis=1), value[24:56])
+
+    def send_halo(k):
         for copy in halo_copies(k):
             copy.start()
 
@@ -230,7 +231,7 @@
                         for i in range(3):
                             total[i] = total[i] + star[g * 3 + i, q, d : d + 1, lanes] * value
                 for i in range(3):
-                    store(g * 3 + i, lanes, total[i])
+                    store(g * 3 + i, l, lanes, total[i])
             return 0
 
         lax.fori_loop(0, 3, one, 0)
@@ -238,21 +239,50 @@
     def taylor(k):
         star_products(s4, lambda q: x[k - 1, q])
 
-        def store(p, lanes, value):
+        def store(p, l, lanes, value):
             x[k, p, :, lanes] = value
+            pack_halo(k, p, l, value)
 
         star_sum(store)
 
     for copy in in_copies[:2]:
         copy.wait()
+    for q in range(Q):
+        for l in range(2):
+            pack_halo(0, q, l, x[0, q, :, l * 128 : (l + 1) * 128])
     taylor(1)
     pl.semaphore_wait(barrier, n - 1)
-    pack_halo(0)
-    pack_halo(1)
+    send_halo(0)
     send(bq, rq, 1, 0)
-    for k in range(2, ORD):
+    send_halo(1)
+    for k in range(2, ORD - 1):
         taylor(k)
-        pack_halo(k)
+        send_halo(k)
+
+    taylor(ORD - 1)
+    send_halo(ORD - 1)
+
+    level = cluster[...]
+
+    def by_level(values):
+        out = jnp.full((1, E), values[0], F32)
+        for c in range(1, NC):
+            out = jnp.where(level == c, values[c], out)
+        return out
+
+    step = by_level(TAUS)
+    own_w = [by_level([WEIGHTS[c][k] for c in range(NC)]) for k in range(ORD)]
+
+    def own_term(q, _):
+        total = own_w[0] * x[0, q]
+        for k in range(1, ORD):
+            total = total + own_w[k] * x[k, q]
+        wrapped = stacked(total)
+        st[q] = dot(st4[...], wrapped)[0 : 3 * B]
+        of[q] = dot(f4[...], wrapped)
+        return 0
+
+    lax.fori_loop(0, Q, own_term, 0, unroll=3)
 
     arrive(bq, rq, 1, 0)
     wanted = (iota((n, E), 1) + 1).astype(F32)
@@ -262,29 +292,6 @@
     for r in range(2):
         bp[pl.ds(r, n, stride=2), :] = answer[r * n : (r + 1) * n]
     send(bp, rp, 2, 1)
-
-    level = cluster[...]
-
-    def by_level(values):
-        out = jnp.full((1, E), values[0], F32)
-        for c in range(1, NC):
-            out = jnp.where(level == c, values[c], out)
-        return out
-
-    step = by_level(TAUS)
-    own_w = [by_level([WEIGHTS[c][k] for c in range(NC)]) for k in range(ORD)]
-
-    def own_term(q, _):
-        total = own_w[0] * x[0, q]
-        for k in range(1, ORD):
-            total = total + own_w[k] * x[k, q]
-        wrapped = stacked(total)
-        st[q] = dot(st4[...], wrapped)[0 : 3 * B]
-        of[q] = dot(f4[...], wrapped)
-        return 0
-
-    lax.fori_loop(0, Q, own_term, 0, unroll=3)
-
     number = nbr[...] - me * E
     ext = jnp.where(number < RIM, number + E, jnp.where(number >= E + RIM, number, number - RIM))
     column = level * EXT + ext
@@ -318,16 +325,14 @@
         for copy in halo_copies(k):
             copy.wait_recv()
 
-    for q in range(5):
-        first, second = [], []
+    for q in range(Q):
+        terms = []
         for k in range(ORD):
             a, b = hrl[k, q], hrr[k, q]
-            first.append(jnp.where(keep, jnp.where(low_half, a, pltpu.roll(b, RIM, axis=1)), 0.0))
-            if q + 5 < Q:
-                second.append(jnp.where(keep, jnp.where(low_half, pltpu.roll(a, RIM, axis=1), b), 0.0))
-        cluster_sums(first, ORDER.index(q), 2)
-        if q + 5 < Q:
-            cluster_sums(second, ORDER.index(q + 5), 2)
+            top = jnp.where(keep, jnp.where(low_half, a, pltpu.roll(b, RIM, axis=1)), 0.0)
+            bottom = jnp.where(keep, jnp.where(low_half, pltpu.roll(a, RIM, axis=1), b), 0.0)
+            terms.append(jnp.concatenate([top, bottom[8:32]], axis=0))
+        cluster_sums(terms, ORDER.index(q), 2)
 
     def gather(start, stop):
         def one(f, _):
@@ -397,7 +402,7 @@
     for q in ORDER[3:]:
         project(q)
 
-    def store_volume(p, lanes, value):
+    def store_volume(p, _, lanes, value):
         acc[p, :, lanes] = x[0, p, :, lanes] + value
 
     star_sum(store_volume)
@@ -447,8 +452,8 @@
 def local(*args):
     (elem_dofs, star_mats, flux_solver, stiffness, face_proj, lift_mats, neighbours, neighbour_face,
      cluster, fault_elem, fault_face, fault_target, fault_params, fault_state) = args
-    vmem, hbm = pl.BlockSpec(memory_space=pltpu.VMEM), pl.BlockSpec(memory_space=pl.ANY)
-    halo = pltpu.VMEM((ORD, 5, B, 128), F32)
+    vmem, hbm = pl.BlockSpec(memory_space=pltpu.VMEM), pl.BlockSpec(memory_space=pltpu.HBM)
+    halo = pltpu.VMEM((ORD, Q, 32, 128), F32)
     small = pltpu.VMEM((N, 128), F32)
     double = pltpu.VMEM((2 * N, 128), F32)
     faces = pltpu.VMEM((Q, NF * GP, E), F32)
@@ -501,9 +506,9 @@
             pltpu.SemaphoreType.DMA((3,)),
         ],
         compiler_params=pltpu.CompilerParams(
-            collective_id=0, has_side_effects=True, vmem_limit_bytes=60 * 1024 * 1024
+            collective_id=0, has_side_effects=True, vmem_limit_bytes=48 * 1024 * 1024
         ),
-    )(
+    )(*[pltpu.with_memory_space_constraint(v, pltpu.HBM) for v in (
         jnp.transpose(elem_dofs, (1, 0, 2)),
         jnp.transpose(star_mats, (1, 2, 0, 3)),
         jnp.transpose(flux_solver, (0, 2, 3, 1, 4)),
@@ -518,7 +523,7 @@
         fault_target.reshape(1, E),
         fault_params,
         fault_state,
-    )
+    )])
     return jnp.transpose(out, (1, 0, 2)), slip, state
 
 

time: 42.6 us -> 39.9 us (0.937)
  Pallas kernels: 38.5 us -> 36.9 us
  local copies, waits for them, and re-layouts: 3.23 us -> 2 us
    pallas_call x1, Pallas kernels: 38.5 us -> 36.9 us  [local(): pl.pallas_call(kernel, out_shape=(jax.ShapeDtypeStruct((Q, B, E), F32), j...]
    unnamed x7 -> x3, local copies, waits for them, and re-layouts: 3.23 us -> 2 us
where the time goes in v4:
time: 39.9 us; the launch traced here: 39.5 us
  Pallas kernels  36.9 us (92%)
  local copies, waits for them, and re-layouts  2 us (5%)
  between operations  0.65 us (2%)
    pallas_call x1, Pallas kernels, local(): pl.pallas_call(kernel, out_shape=(jax.ShapeDtypeStruct((Q, B, E), F32), j...  36.9 us
    unnamed x3, local copies, waits for them, and re-layouts  2 us

profile of v4, /device:TPU:1, one launch (start us, length us, event | category | flops | bytes accessed | tf_op | source)
XLA Modules:
  0.0 39.5 jit_solution(13919639958769518666)
XLA Ops:
  0.6 36.9 %shard_map.157 = (f32[9,56,256]{2,1,0:T(8,128)S(1)}, f32[21,256]{1,0:T(8,128)S(1)}, f32[21,256]{1,0:T(8,128)S(1)}) custom-call(f32[9,56,256]{2,1,0:T(8,128)} %bitcast.12, f32[9,9,3,256]{3,2,1,0:T(4,128)} %bitcast.13, f32[2,9,9,4,256]{4,3,2,1,0:T(4,128)} %bitcast.11, f32[3,56,56]{2,1,0:T(8,128)} %rest_0_.1, f32[21,4,56]{2,1,0:T(4,128)} %bitcast.14, ...), custom_call_target="tpu_custom_call" | custom-call | tf_op jit(solution)/shard_map/pallas_call | solution.py:462
  37.5 0.8 %copy.20 = f32[56,9,256]{2,0,1:T(8,128)} copy(f32[56,9,256]{2,0,1:T(8,128)S(1)} %bitcast.10) | data formatting | bytes 1032192
  38.3 0.6 %copy.21 = f32[21,256]{1,0:T(8,128)} copy(f32[21,256]{1,0:T(8,128)S(1)} %get-tuple-element.13) | data formatting | bytes 43008
  38.9 0.6 %copy.22 = f32[21,256]{1,0:T(8,128)} copy(f32[21,256]{1,0:T(8,128)S(1)} %get-tuple-element.14) | data formatting | bytes 43008

commit v5 on v4

--- a/solution.py
+++ b/solution.py
@@ -48,12 +48,9 @@
     return high, x - high
 
 
-def split3(x):
+def pieces(x):
     high = x.astype(BF16)
-    rest = x - high.astype(F32)
-    mid = rest.astype(BF16)
-    low = (rest - mid.astype(F32)).astype(BF16)
-    return high, mid, low
+    return high, (x - high.astype(F32)).astype(BF16)
 
 
 def stacked(x):
@@ -288,7 +285,7 @@
     wanted = (iota((n, E), 1) + 1).astype(F32)
     for r in range(2):
         own_of[r * n : (r + 1) * n, :] = jnp.where(rq[:, r : r + 1] == wanted, 1.0, 0.0).astype(BF16)
-    answer = sum(dot_nt(own_of[...], piece) for piece in split3(pp[...]))
+    answer = sum(dot_nt(own_of[...], piece) for piece in pieces(pp[...]))
     for r in range(2):
         bp[pl.ds(r, n, stride=2), :] = answer[r * n : (r + 1) * n]
     send(bp, rp, 2, 1)
@@ -358,10 +355,10 @@
 
     arrive(bp, rp, 2, 1)
     given = jnp.concatenate([rp[pl.ds(r, n, stride=2), :] for r in range(2)], axis=0)
-    by_slot = sum(dot(piece, mem[...]) for piece in split3(jnp.transpose(given)))
+    by_slot = sum(dot(piece, mem[...]) for piece in pieces(jnp.transpose(given)))
     by_slot = jnp.where(iota((128, E), 0) == 96, 1.0, by_slot)
     slot_state = by_slot[72:96]
-    slot_pieces = split3(by_slot)
+    slot_pieces = pieces(by_slot)
     slips = []
     for f in range(NF):
         table = etab[f * E : (f + 1) * E, :]
@@ -385,7 +382,7 @@
         traction = locked - imp * slip
         nb[3, rows, :] = jnp.where(here, step * traction, nb[3, rows, :])
         nb[7, rows, :] = jnp.where(here, step * (inner[2] + slip), nb[7, rows, :])
-        slips.append(split3(jnp.where(here, slip, 0.0)))
+        slips.append(pieces(jnp.where(here, slip, 0.0)))
     slot_slip = jnp.zeros((24, E), F32)
     for f in range(NF):
         for piece in slips[f]:
@@ -394,7 +391,7 @@
     next_state = STEADY + (slot_state - STEADY) * jnp.exp(-jnp.abs(slot_slip))
     gap8, gap72 = jnp.zeros((8, E), F32), jnp.zeros((72, E), F32)
     wrapped = jnp.concatenate([next_state, gap8, next_state, gap72], axis=0)
-    told = sum(dot_nt(mem[...], piece) for piece in split3(wrapped))
+    told = sum(dot_nt(mem[...], piece) for piece in pieces(wrapped))
     bs[...] = jnp.where(lane2 < 32, told[0:n], told[n : 2 * n])
     send(bs, rs, 1, 2)
 
@@ -437,7 +434,7 @@
     arrive(bs, rs, 1, 2)
     turned = jnp.transpose(rs[...])
     news = jnp.concatenate([turned[0:24], turned[32:56]], axis=1)
-    update = sum(dot(piece, own_of[...]) for piece in split3(news))
+    update = sum(dot(piece, own_of[...]) for piece in pieces(news))
     hit = dot(jnp.ones((16, E), BF16), own_of[...])[0:1] > 0.5
     state_out[...] = jnp.where(hit, update[0:FB], state[...])
 

time: 39.9 us -> 39.7 us (level)
  no operation moved by 1% of the time
where the time goes in v5:
time: 39.7 us; the launch traced here: 39.3 us
  Pallas kernels  36.6 us (92%)
  local copies, waits for them, and re-layouts  2 us (5%)
  between operations  0.65 us (2%)
    pallas_call x1, Pallas kernels, local(): pl.pallas_call(kernel, out_shape=(jax.ShapeDtypeStruct((Q, B, E), F32), j...  36.6 us
    unnamed x3, local copies, waits for them, and re-layouts  2 us

profile of v5, /device:TPU:1, one launch (start us, length us, event | category | flops | bytes accessed | tf_op | source)
XLA Modules:
  0.0 39.3 jit_solution(16284406893305954525)
XLA Ops:
  0.6 36.6 %shard_map.157 = (f32[9,56,256]{2,1,0:T(8,128)S(1)}, f32[21,256]{1,0:T(8,128)S(1)}, f32[21,256]{1,0:T(8,128)S(1)}) custom-call(f32[9,56,256]{2,1,0:T(8,128)} %bitcast.12, f32[9,9,3,256]{3,2,1,0:T(4,128)} %bitcast.13, f32[2,9,9,4,256]{4,3,2,1,0:T(4,128)} %bitcast.11, f32[3,56,56]{2,1,0:T(8,128)} %rest_0_.1, f32[21,4,56]{2,1,0:T(4,128)} %bitcast.14, ...), custom_call_target="tpu_custom_call" | custom-call | tf_op jit(solution)/shard_map/pallas_call | solution.py:459
  37.3 0.8 %copy.20 = f32[56,9,256]{2,0,1:T(8,128)} copy(f32[56,9,256]{2,0,1:T(8,128)S(1)} %bitcast.10) | data formatting | bytes 1032192
  38.1 0.6 %copy.21 = f32[21,256]{1,0:T(8,128)} copy(f32[21,256]{1,0:T(8,128)S(1)} %get-tuple-element.13) | data formatting | bytes 43008
  38.7 0.6 %copy.22 = f32[21,256]{1,0:T(8,128)} copy(f32[21,256]{1,0:T(8,128)S(1)} %get-tuple-element.14) | data formatting | bytes 43008
